TPU v7x, 768 devices: a whole 4x8x12 slice. The times are simulated.
768 devices in a mesh: band: 16 (over y, core), field: 48 (over x, z).
Axes of the slice: x: 4, y: 8, z: 12, core: 2. Of those that a mesh axis runs over, the one named last changes fastest.
Arguments:
- spectra: bfloat16 [256, 2, 192, 1280], P('band', None, 'field'), may hold values from -0.29882812 to 0.29882812
- legendre: bfloat16 [256, 128, 1280], P('band'), may hold values from -0.15625 to 0.15625
- wavenum: int32 [256], replicated, may hold values from 0 to 1279, as said below
- dep_row: int32 [128, 4608], P('band', 'field'), may hold values from 0 to 126, as said below
- dep_col: int32 [128, 4608], P('band', 'field'), may hold values from 0 to 4607, as said below
- frac_row: float32 [128, 4608], P('band', 'field'), may hold values from 0 to 1
- frac_col: float32 [128, 4608], P('band', 'field'), may hold values from 0 to 1
Outputs:
- advected: float32 [192, 128, 4608], P(None, 'band', 'field')
Inputs may be any that keep to these rules, and one draw needn't show every extreme that they name: `wavenum`: strictly increasing; the first slot holds 0 and the last 1279. `dep_row`: for the arrival point in row r the value lies within r - 2 to r + 1. `dep_col`: for the arrival point in column k the value lies cyclically within k - 2 to k + 1 (mod 4608).
All inputs are finite; a program needn't handle non-finite values.
Results may differ from a plain program's by a relative error of at most 0.0043.
Values may be sent and summed in bfloat16 or wider, within the bound.
No kernel may reach another device: no remote copies, remote signals or barrier semaphores. Data moves between devices by JAX's collectives and lax.ppermute only.
A program may use at most 64 MiB of HBM per device.

v0:
```python
import jax
import jax.numpy as jnp
from jax import lax
from jax.sharding import PartitionSpec as P

NLON = 4608
HW = 2


def with_halo(block, sides, width):
    for axis, dim in sides:
        count = lax.axis_size(axis)
        forward = [(i, i + 1) for i in range(count - 1)]
        forward.append((count - 1, 0))
        backward = [(target, source) for source, target in forward]
        low = lax.ppermute(
            lax.slice_in_dim(block, block.shape[dim] - width, None, axis=dim), axis, forward
        )
        high = lax.ppermute(lax.slice_in_dim(block, 0, width, axis=dim), axis, backward)
        block = jnp.concatenate([low, block, high], axis=dim)
    return block


def fourier_table(wavenum, nlon):
    points = lax.iota(jnp.int32, nlon)
    phase = wavenum[:, None] * points[None, :] % nlon
    angle = phase.astype(jnp.float32) * (2.0 * 3.141592653589793 / nlon)
    weight = jnp.where(wavenum == 0, 1.0, 2.0).astype(jnp.float32)[:, None]
    return jnp.stack([weight * jnp.cos(angle), -weight * jnp.sin(angle)], axis=1).astype(
        jnp.bfloat16
    )


def local(spectra, legendre, wavenum, dep_row, dep_col, frac_row, frac_col):
    band_index = lax.axis_index("band")
    field_index = lax.axis_index("field")
    band_count = lax.axis_size("band")
    field_count = lax.axis_size("field")
    slots = spectra.shape[0]
    local_fields = spectra.shape[2]
    degrees = spectra.shape[3]
    lat_all = legendre.shape[1]
    lat_band = lat_all // band_count
    seg_width = NLON // field_count
    local_wave = lax.dynamic_slice_in_dim(wavenum, band_index * slots, slots)
    valid = degrees - local_wave
    width = min(256, degrees)
    turns = (jnp.max(valid) + width - 1) // width

    def legendre_block(turn, total):
        start = turn * width
        spec_part = lax.dynamic_slice_in_dim(spectra, start, width, 3)
        table_part = lax.dynamic_slice_in_dim(legendre, start, width, 2)
        position = start + lax.iota(jnp.int32, width)
        keep = position[None, :] < valid[:, None]
        spec_part = jnp.where(keep[:, None, None, :], spec_part, jnp.zeros_like(spec_part))
        return total + jnp.einsum(
            "scfj,slj->scfl", spec_part, table_part, preferred_element_type=jnp.float32
        )

    start_total = jnp.zeros((slots, 2, local_fields, lat_all), jnp.float32)
    four = lax.fori_loop(0, turns, legendre_block, start_total).astype(jnp.bfloat16)
    spectral_rows = lax.all_to_all(four, "band", split_axis=3, concat_axis=0, tiled=True)
    all_slots = spectral_rows.shape[0]
    rows_here = spectral_rows.shape[3]
    table = fourier_table(wavenum, NLON).reshape(all_slots * 2, NLON)
    flat = spectral_rows.reshape(all_slots * 2, local_fields * rows_here)
    grid = lax.dot_general(
        flat, table, (((0,), (0,)), ((), ())), preferred_element_type=jnp.float32
    )
    grid = grid.reshape(local_fields, rows_here, NLON).astype(jnp.bfloat16)
    segment_block = lax.all_to_all(grid, "field", split_axis=2, concat_axis=0, tiled=True)
    extended = with_halo(segment_block, (("field", 2),), HW)
    extended = with_halo(extended, (("band", 1),), HW)
    values = extended.astype(jnp.float32)
    row_ids = band_index * lat_band + lax.broadcasted_iota(jnp.int32, dep_row.shape, 0)
    col_ids = field_index * seg_width + lax.broadcasted_iota(jnp.int32, dep_col.shape, 1)
    delta_row = dep_row - row_ids
    delta_col = (dep_col - col_ids + HW) % NLON - HW
    zero_plane = jnp.zeros_like(frac_row)
    col_weights = []
    for offset_col in range(-HW, HW + 1):
        col_weights.append(
            jnp.where(delta_col == offset_col, 1.0 - frac_col, zero_plane)
            + jnp.where(delta_col + 1 == offset_col, frac_col, zero_plane)
        )
    result = jnp.zeros((values.shape[0],) + dep_row.shape, jnp.float32)
    for offset_row in range(-HW, HW + 1):
        row_weight = jnp.where(delta_row == offset_row, 1.0 - frac_row, zero_plane) + jnp.where(
            delta_row + 1 == offset_row, frac_row, zero_plane
        )
        first_row = HW + offset_row
        inner_sum = jnp.zeros_like(result)
        for index_col in range(2 * HW + 1):
            window = values[:, first_row : first_row + lat_band, index_col : index_col + seg_width]
            inner_sum = inner_sum + (row_weight * col_weights[index_col])[None, :, :] * window
        result = result + inner_sum
    return result


def solution(mesh):
    return jax.shard_map(
        local,
        mesh=mesh,
        in_specs=(
            P("band", None, "field", None),
            P("band", None, None),
            P(),
            P("band", "field"),
            P("band", "field"),
            P("band", "field"),
            P("band", "field"),
        ),
        out_specs=P(None, "band", "field"),
        check_vma=False,
    )
```

profile of v0, /device:TPU:1, one launch (start us, length us, event | category | flops | bytes accessed | tf_op | source)
XLA Modules:
  0.0 154.1 jit_solution(405803417377234307)
XLA Ops:
  0.0 1.5 fusion.48
  2.3 8.8 %while.10 = (s32[]{:T(128)}, f32[16,2,4,128]{3,2,1,0:T(4,128)S(1)}, s32[]{:T(128)}, s32[16]{0:T(128)S(1)}, bf16[16,2,4,1280]{3,2,1,0:T(4,128)(2,1)}, /*index=5*/...) while((s32[]{:T(128)}, f32[16,2,4,128]{3,2,1,0:T(4,128)S(1)}, s32[]{:T(128)}, ...), condition=%wide.region_2.3_spmd, body=%wide.region_1.2_spmd.sunk | while | flops 8442118 | bytes 1256671 | solution.py:62
  2.4 1.7 %convolution_add_fusion.2 = f32[16,2,4,128]{3,2,1,0:T(4,128)S(1)} fusion(f32[16,2,4,128]{3,2,1,0:T(4,128)S(1)} %get-tuple-element.165, bf16[16,128,1280]{2,1,0:T(8,128)(2,1)} %get-tuple-element.179, s32[]{:T(128)S(6)} %select_n.202, bf16[16,2,4,1280]{3,2,1,0:T(4,128)(2,1)} %get-tuple-element.178, pred[16,256]{1,0:T(8,128)(4,1)S(1)} %broadcast_compare_fusion.2), kind=kOutput, calls=%fused_computation.clone.1 | convolution fusion | flops 8437760 | bytes 1250304 | tf_op jit(solution)/shard_map/while/body/scfj,slj->scfl/dot_general | solution.py:57
  4.1 1.7 %convolution_add_fusion.2 = f32[16,2,4,128]{3,2,1,0:T(4,128)S(1)} fusion(f32[16,2,4,128]{3,2,1,0:T(4,128)S(1)} %get-tuple-element.165, bf16[16,128,1280]{2,1,0:T(8,128)(2,1)} %get-tuple-element.179, s32[]{:T(128)S(6)} %select_n.202, bf16[16,2,4,1280]{3,2,1,0:T(4,128)(2,1)} %get-tuple-element.178, pred[16,256]{1,0:T(8,128)(4,1)S(1)} %broadcast_compare_fusion.2), kind=kOutput, calls=%fused_computation.clone.1 | convolution fusion | flops 8437760 | bytes 1250304 | tf_op jit(solution)/shard_map/while/body/scfj,slj->scfl/dot_general | solution.py:57
  5.9 1.7 %convolution_add_fusion.2 = f32[16,2,4,128]{3,2,1,0:T(4,128)S(1)} fusion(f32[16,2,4,128]{3,2,1,0:T(4,128)S(1)} %get-tuple-element.165, bf16[16,128,1280]{2,1,0:T(8,128)(2,1)} %get-tuple-element.179, s32[]{:T(128)S(6)} %select_n.202, bf16[16,2,4,1280]{3,2,1,0:T(4,128)(2,1)} %get-tuple-element.178, pred[16,256]{1,0:T(8,128)(4,1)S(1)} %broadcast_compare_fusion.2), kind=kOutput, calls=%fused_computation.clone.1 | convolution fusion | flops 8437760 | bytes 1250304 | tf_op jit(solution)/shard_map/while/body/scfj,slj->scfl/dot_general | solution.py:57
  7.6 1.7 %convolution_add_fusion.2 = f32[16,2,4,128]{3,2,1,0:T(4,128)S(1)} fusion(f32[16,2,4,128]{3,2,1,0:T(4,128)S(1)} %get-tuple-element.165, bf16[16,128,1280]{2,1,0:T(8,128)(2,1)} %get-tuple-element.179, s32[]{:T(128)S(6)} %select_n.202, bf16[16,2,4,1280]{3,2,1,0:T(4,128)(2,1)} %get-tuple-element.178, pred[16,256]{1,0:T(8,128)(4,1)S(1)} %broadcast_compare_fusion.2), kind=kOutput, calls=%fused_computation.clone.1 | convolution fusion | flops 8437760 | bytes 1250304 | tf_op jit(solution)/shard_map/while/body/scfj,slj->scfl/dot_general | solution.py:57
  9.4 1.7 %convolution_add_fusion.2 = f32[16,2,4,128]{3,2,1,0:T(4,128)S(1)} fusion(f32[16,2,4,128]{3,2,1,0:T(4,128)S(1)} %get-tuple-element.165, bf16[16,128,1280]{2,1,0:T(8,128)(2,1)} %get-tuple-element.179, s32[]{:T(128)S(6)} %select_n.202, bf16[16,2,4,1280]{3,2,1,0:T(4,128)(2,1)} %get-tuple-element.178, pred[16,256]{1,0:T(8,128)(4,1)S(1)} %broadcast_compare_fusion.2), kind=kOutput, calls=%fused_computation.clone.1 | convolution fusion | flops 8437760 | bytes 1250304 | tf_op jit(solution)/shard_map/while/body/scfj,slj->scfl/dot_general | solution.py:57
  11.3 0.9 reshape.190
  12.2 13.8 %all-to-all-start = ((bf16[16,2,512]{2,1,0:T(2,128)(2,1)}), bf16[16,2,512]{2,1,0:T(2,128)(2,1)S(1)}, u32[]{:S(2)}, u32[]{:S(2)}) async-start(bf16[16,2,512]{2,1,0:T(2,128)(2,1)} %reshape.190), calls=%async_computation | async-start | bytes 65536 | tf_op jit(solution)/shard_map/all_to_all | solution.py:63
  26.0 20.9 %multiply_convert_fusion.1 = (bf16[256,1,4608]{2,0,1:T(8,128)(2,1)S(1)}, bf16[256,1,4608]{2,0,1:T(8,128)(2,1)S(1)}) fusion(s32[256]{0:T(256)S(1)} %copy-done.4, f32[256]{0:T(256)S(1)} %get-tuple-element.106, f32[256]{0:T(256)S(1)} %get-tuple-element.107), kind=kLoop, calls=%fused_computation.17 | loop fusion | flops 15335424 | bytes 4721664 | tf_op jit(solution)/shard_map/convert
  46.9 2.6 %pad_maximum_fusion = bf16[256,2,4608]{2,0,1:T(8,128)(2,1)} fusion(bf16[256,1,4608]{2,0,1:T(8,128)(2,1)S(1)} %get-tuple-element.105, bf16[256,1,4608]{2,0,1:T(8,128)(2,1)S(1)} %get-tuple-element.104), kind=kLoop, calls=%fused_computation.15 | loop fusion | flops 2359296 | bytes 9437184 | tf_op jit(solution)/shard_map/stack | solution.py:29
  49.5 9.3 %copy.30 = bf16[256,2,4608]{2,1,0:T(2,128)(2,1)} copy(bf16[256,2,4608]{2,0,1:T(8,128)(2,1)} %pad_maximum_fusion) | data formatting | bytes 9437184 | tf_op jit(solution)/shard_map/stack | solution.py:29
  58.8 7.5 %reshape.188 = bf16[512,4608,1]{1,0,2:T(8,128)(2,1)} reshape(bf16[256,2,4608]{2,1,0:T(2,128)(2,1)} %copy.30) | data formatting | bytes 9437184 | tf_op jit(solution)/shard_map/convert_element_type | solution.py:29
  66.6 0.4 copy.28
  67.0 0.3 reshape.186
  67.4 3.2 %convolution_convert_fusion = bf16[4,8,4608]{2,1,0:T(8,128)(2,1)S(1)} fusion(bf16[512,4608,1]{1,0,2:T(8,128)(2,1)} %reshape.188, bf16[32,512]{1,0:T(8,128)(2,1)S(1)} %copy.29), kind=kOutput, calls=%fused_computation.12 | convolution fusion | flops 151142400 | bytes 5046272 | tf_op jit(solution)/shard_map/dot_general | solution.py:68
  70.6 4.9 %copy.31 = bf16[4,8,4608]{1,0,2:T(4,128)(2,1)} copy(bf16[4,8,4608]{2,1,0:T(8,128)(2,1)S(1)} %convolution_convert_fusion) | data formatting | bytes 589824 | tf_op jit(solution)/shard_map/convert_element_type | solution.py:71
  75.5 11.3 %reshape.192 = bf16[48,2,1536]{2,1,0:T(2,128)(2,1)} reshape(bf16[4608,4,8]{2,1,0:T(4,128)(2,1)} %bitcast.25) | data formatting | bytes 589824
  86.8 9.3 %all-to-all-start.1 = ((bf16[48,2,1536]{2,1,0:T(2,128)(2,1)}), bf16[48,2,1536]{2,1,0:T(2,128)(2,1)S(1)}, u32[]{:S(2)}, u32[]{:S(2)}) async-start(bf16[48,2,1536]{2,1,0:T(2,128)(2,1)} %reshape.192), calls=%async_computation.1 | async-start | bytes 589824 | tf_op jit(solution)/shard_map/all_to_all | solution.py:72
  96.3 16.5 %all-to-all-done.1 = bf16[48,2,1536]{2,1,0:T(2,128)(2,1)S(1)} async-done(((bf16[48,2,1536]{2,1,0:T(2,128)(2,1)}), bf16[48,2,1536]{2,1,0:T(2,128)(2,1)S(1)}, u32[]{:S(2)}, u32[]{:S(2)}) %all-to-all-start.1) | async-done | bytes 294944 | tf_op jit(solution)/shard_map/all_to_all | solution.py:72
  112.8 6.6 %reshape.193 = bf16[4608,4,8]{2,1,0:T(4,128)(2,1)} reshape(bf16[48,2,1536]{2,1,0:T(2,128)(2,1)S(1)} %all-to-all-done.1) | data formatting | bytes 589824
  119.4 5.5 %copy.32 = bf16[48,4,8,96]{3,2,1,0:T(8,128)(2,1)S(1)} copy(bf16[48,4,8,96]{2,1,3,0:T(4,128)(2,1)} %bitcast.26) | data formatting | bytes 589824 | tf_op jit(solution)/shard_map/all_to_all | solution.py:72
  125.1 2.2 %collective-permute-start.1 = (bf16[192,8,2]{2,1,0:T(8,128)(2,1)S(1)}, bf16[192,8,2]{2,1,0:T(8,128)(2,1)S(1)}, u32[]{:S(2)}, u32[]{:S(2)}) collective-permute-start(bf16[192,8,2]{2,1,0:T(8,128)(2,1)S(1)} %get-tuple-element.75), channel_id=1, source_target_pairs={{1,0},{2,1},{3,2},{4,3},{5,4},{6,5},{7,6},{8,7},{9,8},{10,9},{11,1... | collective-permute-start | bytes 18440 | tf_op jit(solution)/shard_map/ppermute | solution.py:19
  127.3 3.1 %collective-permute-start = (bf16[192,8,2]{2,1,0:T(8,128)(2,1)S(1)}, bf16[192,8,2]{2,1,0:T(8,128)(2,1)S(1)}, u32[]{:S(2)}, u32[]{:S(2)}) collective-permute-start(bf16[192,8,2]{2,1,0:T(8,128)(2,1)S(1)} %get-tuple-element.74), channel_id=1, source_target_pairs={{0,1},{1,2},{2,3},{3,4},{4,5},{5,6},{6,7},{7,8},{8,9},{9,10},{10,1... | collective-permute-start | bytes 18440 | tf_op jit(solution)/shard_map/ppermute | solution.py:16
  130.5 4.5 %collective-permute-done.1 = bf16[192,8,2]{2,1,0:T(8,128)(2,1)S(1)} collective-permute-done((bf16[192,8,2]{2,1,0:T(8,128)(2,1)S(1)}, bf16[192,8,2]{2,1,0:T(8,128)(2,1)S(1)}, u32[]{:S(2)}, u32[]{:S(2)}) %collective-permute-start.1) | collective-permute-done | bytes 6176 | tf_op jit(solution)/shard_map/ppermute | solution.py:19
  135.0 5.0 %collective-permute-done = bf16[192,8,2]{2,1,0:T(8,128)(2,1)S(1)} collective-permute-done((bf16[192,8,2]{2,1,0:T(8,128)(2,1)S(1)}, bf16[192,8,2]{2,1,0:T(8,128)(2,1)S(1)}, u32[]{:S(2)}, u32[]{:S(2)}) %collective-permute-start) | collective-permute-done | bytes 6176 | tf_op jit(solution)/shard_map/ppermute | solution.py:16
  140.0 0.7 pad_maximum_fusion.3
  140.7 4.0 %collective-permute-start.3 = (bf16[192,2,100]{2,1,0:T(2,128)(2,1)S(1)}, bf16[192,2,100]{2,1,0:T(2,128)(2,1)S(1)}, u32[]{:S(2)}, u32[]{:S(2)}) collective-permute-start(bf16[192,2,100]{2,1,0:T(2,128)(2,1)S(1)} %get-tuple-element.73), channel_id=1, source_target_pairs={{48,0},{96,48},{144,96},{192,144},{240,192},{288,240},{336,288},{3... | collective-permute-start | bytes 230408 | tf_op jit(solution)/shard_map/ppermute | solution.py:19
  144.8 0.9 collective-permute-start.2
  145.6 2.3 %collective-permute-done.3 = bf16[192,2,100]{2,1,0:T(2,128)(2,1)S(1)} collective-permute-done((bf16[192,2,100]{2,1,0:T(2,128)(2,1)S(1)}, bf16[192,2,100]{2,1,0:T(2,128)(2,1)S(1)}, u32[]{:S(2)}, u32[]{:S(2)}) %collective-permute-start.3) | collective-permute-done | bytes 76832 | tf_op jit(solution)/shard_map/ppermute | solution.py:19
  147.9 1.2 maximum_convert_fusion
  149.1 5.0 %fusion.14 = f32[192,8,96]{2,1,0:T(8,128)} fusion(f32[192,12,100]{2,1,0:T(8,128)S(1)} %maximum_convert_fusion, f32[8,96]{1,0:T(8,128)S(1)} %get-tuple-element.100, f32[8,96]{1,0:T(8,128)S(1)} %get-tuple-element.98, f32[8,96]{1,0:T(8,128)S(1)} %get-tuple-element.97, f32[8,96]{1,0:T(8,128)S(1)} %get-tuple-element.99, f32[8,96]{1,0:T(8,128)S(1)} %get-tuple-element.108, ...), kind=kLoop, calls=%fused_computation.24 | loop fusion | flops 7225344 | bytes 15412224 | tf_op jit(solution)/shard_map/add | solution.py:97
  (35 shorter events, 1.3 us)
Async XLA Ops:
  0.0 26.0 %copy-start.4 = (s32[256]{0:T(256)S(1)}, s32[256]{0:T(256)}, u32[]{:S(2)}) copy-start(s32[256]{0:T(256)} %param.11) | copy-start | bytes 3076
  12.2 54.2 %all-to-all-start = ((bf16[16,2,512]{2,1,0:T(2,128)(2,1)}), bf16[16,2,512]{2,1,0:T(2,128)(2,1)S(1)}, u32[]{:S(2)}, u32[]{:S(2)}) async-start(bf16[16,2,512]{2,1,0:T(2,128)(2,1)} %reshape.190), calls=%async_computation | async-start | bytes 65536 | tf_op jit(solution)/shard_map/all_to_all | solution.py:63
  70.6 25.6 %copy-start = (f32[8,96]{1,0:T(8,128)S(1)}, f32[8,96]{1,0:T(8,128)}, u32[]{:S(2)}) copy-start(f32[8,96]{1,0:T(8,128)} %param.14) | copy-start | bytes 9220
  70.6 25.6 %copy-start.1 = (s32[8,96]{1,0:T(8,128)S(1)}, s32[8,96]{1,0:T(8,128)}, u32[]{:S(2)}) copy-start(s32[8,96]{1,0:T(8,128)} %param.12) | copy-start | bytes 9220
  70.6 25.6 %copy-start.2 = (f32[8,96]{1,0:T(8,128)S(1)}, f32[8,96]{1,0:T(8,128)}, u32[]{:S(2)}) copy-start(f32[8,96]{1,0:T(8,128)} %param.15) | copy-start | bytes 9220
  70.6 25.6 %copy-start.3 = (s32[8,96]{1,0:T(8,128)S(1)}, s32[8,96]{1,0:T(8,128)}, u32[]{:S(2)}) copy-start(s32[8,96]{1,0:T(8,128)} %param.13) | copy-start | bytes 9220
  86.8 26.0 %all-to-all-start.1 = ((bf16[48,2,1536]{2,1,0:T(2,128)(2,1)}), bf16[48,2,1536]{2,1,0:T(2,128)(2,1)S(1)}, u32[]{:S(2)}, u32[]{:S(2)}) async-start(bf16[48,2,1536]{2,1,0:T(2,128)(2,1)} %reshape.192), calls=%async_computation.1 | async-start | bytes 589824 | tf_op jit(solution)/shard_map/all_to_all | solution.py:72
  125.1 9.9 %collective-permute-start.1 = (bf16[192,8,2]{2,1,0:T(8,128)(2,1)S(1)}, bf16[192,8,2]{2,1,0:T(8,128)(2,1)S(1)}, u32[]{:S(2)}, u32[]{:S(2)}) collective-permute-start(bf16[192,8,2]{2,1,0:T(8,128)(2,1)S(1)} %get-tuple-element.75), channel_id=1, source_target_pairs={{1,0},{2,1},{3,2},{4,3},{5,4},{6,5},{7,6},{8,7},{9,8},{10,9},{11,1... | collective-permute-start | bytes 18440 | tf_op jit(solution)/shard_map/ppermute | solution.py:19
  127.3 12.7 %collective-permute-start = (bf16[192,8,2]{2,1,0:T(8,128)(2,1)S(1)}, bf16[192,8,2]{2,1,0:T(8,128)(2,1)S(1)}, u32[]{:S(2)}, u32[]{:S(2)}) collective-permute-start(bf16[192,8,2]{2,1,0:T(8,128)(2,1)S(1)} %get-tuple-element.74), channel_id=1, source_target_pairs={{0,1},{1,2},{2,3},{3,4},{4,5},{5,6},{6,7},{7,8},{8,9},{9,10},{10,1... | collective-permute-start | bytes 18440 | tf_op jit(solution)/shard_map/ppermute | solution.py:16
  140.7 7.2 %collective-permute-start.3 = (bf16[192,2,100]{2,1,0:T(2,128)(2,1)S(1)}, bf16[192,2,100]{2,1,0:T(2,128)(2,1)S(1)}, u32[]{:S(2)}, u32[]{:S(2)}) collective-permute-start(bf16[192,2,100]{2,1,0:T(2,128)(2,1)S(1)} %get-tuple-element.73), channel_id=1, source_target_pairs={{48,0},{96,48},{144,96},{192,144},{240,192},{288,240},{336,288},{3... | collective-permute-start | bytes 230408 | tf_op jit(solution)/shard_map/ppermute | solution.py:19
  144.8 3.2 %collective-permute-start.2 = (bf16[192,2,100]{2,1,0:T(2,128)(2,1)S(1)}, bf16[192,2,100]{2,1,0:T(2,128)(2,1)S(1)}, u32[]{:S(2)}, u32[]{:S(2)}) collective-permute-start(bf16[192,2,100]{2,1,0:T(2,128)(2,1)S(1)} %get-tuple-element.72), channel_id=1, source_target_pairs={{0,48},{48,96},{96,144},{144,192},{192,240},{240,288},{288,336},{3... | collective-permute-start | bytes 230408 | tf_op jit(solution)/shard_map/ppermute | solution.py:16
where the time goes:
time: 155 us; the launch traced here: 154 us
  local copies, waits for them, and re-layouts  47.4 us (31%)
  starting transfers between devices  33.3 us (21%)
  other arithmetic  32.5 us (21%)
  waiting for transfers between devices  28.3 us (18%)
  matrix products  11.5 us (7%)
    another operation x1, other arithmetic  20.9 us
    unnamed x14, local copies, waits for them, and re-layouts  19 us
    all_to_all x1, waiting for transfers between devices, local(): lax.all_to_all(grid, 'field', split_axis=2, concat_axis=0, tiled=True)  16.5 us
    all_to_all x1, starting transfers between devices, local(): lax.all_to_all(four, 'band', split_axis=3, concat_axis=0, tiled=True)  13.8 us
    all_to_all x1, starting transfers between devices, local(): lax.all_to_all(grid, 'field', split_axis=2, concat_axis=0, tiled=True)  9.35 us
    another operation x1, local copies, waits for them, and re-layouts, fourier_table(): jnp.stack([weight * jnp.cos(angle), -weight * jnp.sin(angle)], axis=1)  9.31 us
    dot_general x5, matrix products, legendre_block(): jnp.einsum('scfj,slj->scfl', spec_part, table_part, preferred_element_typ...  8.28 us
    convert_element_type x1, local copies, waits for them, and re-layouts, fourier_table(): jnp.stack([weight * jnp.cos(angle), -weight * jnp.sin(angle)], axis=1)  7.54 us
  transfers between devices with their start and end apart: 6, of which 4 were waited for; matrix products, arithmetic and copies ran while one was open for 26% of the time, Pallas kernels for 0%

commit v1 on v0

v1 whole, which is shorter than its diff:
```python
import jax
import jax.numpy as jnp
from jax import lax
from jax.experimental import pallas as pl
from jax.experimental.pallas import tpu as pltpu
from jax.sharding import PartitionSpec as P

NLON = 4608
HW = 2
XS = 4
ZS = 12
J = 3
ZC = ZS // J
PEERS = XS * ZC
TAPS = 2 * HW + 1
WIN = 12
SLAB = 16
LANES = 128
MIB = 1024 * 1024


def legendre_kernel(wave_ref, spec_hbm, leg_hbm, out_ref, spec_buf, leg_buf, pad_ref, spec_sem, leg_sem):
    slots, parts, fields, degrees = spec_buf.shape
    lats = leg_buf.shape[1]
    group = parts * fields
    spec_copy = pltpu.make_async_copy(spec_hbm, spec_buf, spec_sem)
    spec_copy.start()
    leg_copies = [
        pltpu.make_async_copy(leg_hbm.at[s], leg_buf.at[s], leg_sem.at[s]) for s in range(slots)
    ]
    for copy in leg_copies:
        copy.start()
    first = lax.axis_index("band") * slots
    pad_ref[...] = jnp.zeros_like(pad_ref)
    lane_in = lax.broadcasted_iota(jnp.int32, (LANES, LANES), 0)
    lane_out = lax.broadcasted_iota(jnp.int32, (LANES, LANES), 1)
    order = (lane_in % fields) * (LANES // fields) + lane_in // fields
    perm = jnp.where(order == lane_out, 1.0, 0.0).astype(jnp.bfloat16)
    position = lax.broadcasted_iota(jnp.int32, (group, degrees), 1)
    zeros8 = jnp.zeros((group, degrees), jnp.float32)
    spec_copy.wait()
    total = jnp.zeros((lats, LANES), jnp.float32)
    for s in range(slots):
        part = spec_buf[s].astype(jnp.float32)
        rows = jnp.concatenate([part[0], part[1]], axis=0)
        rows = jnp.where(position < degrees - wave_ref[first + s], rows, 0.0)
        pair = [rows, zeros8] if s % 2 == 0 else [zeros8, rows]
        tile = jnp.concatenate(pair, axis=0).astype(jnp.bfloat16)
        pieces = []
        if s // 2 > 0:
            pieces.append(jnp.zeros((2 * group * (s // 2), degrees), jnp.bfloat16))
        pieces.append(tile)
        if s // 2 < slots // 2 - 1:
            pieces.append(
                jnp.zeros((2 * group * (slots // 2 - 1 - s // 2), degrees), jnp.bfloat16)
            )
        weights = jnp.concatenate(pieces, axis=0)
        leg_copies[s].wait()
        total = total + lax.dot_general(
            leg_buf[s], weights, (((1,), (1,)), ((), ())), preferred_element_type=jnp.float32
        )
    four = jnp.dot(total.astype(jnp.bfloat16), perm, preferred_element_type=jnp.float32)
    pad_ref[HW : HW + lats, :] = four
    bands = out_ref.shape[0] // J
    for b in range(bands):
        tile = pad_ref[b * (lats // bands) : b * (lats // bands) + SLAB, :].astype(jnp.bfloat16)
        for j in range(J):
            out_ref[b * J + j] = tile


def reduced_angle(product):
    turns = jnp.floor(product * (1.0 / NLON))
    return (product - turns * NLON) * (2.0 * 3.141592653589793 / NLON)


def table_kernel(wave_ref, start_ref, out_ref):
    rows = out_ref.shape[0]
    wave = wave_ref[...]
    lane = lax.broadcasted_iota(jnp.int32, (rows, LANES), 1).astype(jnp.float32)
    part = (lax.broadcasted_iota(jnp.int32, (rows, LANES), 0) % 2).astype(jnp.float32)
    weight = jnp.where(wave == 0.0, 1.0, 2.0)
    inner = reduced_angle(wave * lane)
    outer = reduced_angle(wave * start_ref[...] + part * (NLON // 4))
    cos_in, sin_in = jnp.cos(inner), jnp.sin(inner)
    cos_out, sin_out = weight * jnp.cos(outer), weight * jnp.sin(outer)
    for p in range(PEERS):
        out_ref[:, p * LANES : (p + 1) * LANES] = (
            cos_out[:, p : p + 1] * cos_in - sin_out[:, p : p + 1] * sin_in
        ).astype(jnp.bfloat16)


def fourier_kernel(four_ref, table_ref, out_ref, flat_ref):
    bands = four_ref.shape[0] // J
    width = 32
    fields = LANES // width
    per_tile = LANES // width
    for j in range(J):
        for q in range(bands // per_tile):
            blocks = [
                four_ref[(per_tile * q + i) * J + j].astype(jnp.float32) for i in range(per_tile)
            ]
            for f in range(fields):
                piece = jnp.concatenate(
                    [block[:WIN, f * width : (f + 1) * width] for block in blocks], axis=1
                )
                row = (j * fields + f) * WIN
                flat_ref[row : row + WIN, q * LANES : (q + 1) * LANES] = piece
    flat = flat_ref[...].astype(jnp.bfloat16)
    for n in range(PEERS // 2):
        grid = jnp.dot(
            flat,
            table_ref[:, 2 * n * LANES : 2 * (n + 1) * LANES],
            preferred_element_type=jnp.float32,
        ).astype(jnp.bfloat16)
        out_ref[2 * n] = grid[:, :LANES]
        out_ref[2 * n + 1] = grid[:, LANES:]


def interp_kernel(grid_ref, dep_row, dep_col, frac_row, frac_col, out_ref, buf, weight_ref):
    rows, cols = dep_row.shape
    fields = 4
    row_ids = lax.axis_index("band") * rows + lax.broadcasted_iota(jnp.int32, (rows, cols), 0)
    col_ids = lax.axis_index("field") * cols + lax.broadcasted_iota(jnp.int32, (rows, cols), 1)
    delta_row = dep_row[...] - row_ids
    delta_col = dep_col[...] - col_ids + HW
    delta_col = jnp.where(delta_col < 0, delta_col + NLON, delta_col)
    delta_col = jnp.where(delta_col >= NLON, delta_col - NLON, delta_col) - HW
    a = frac_row[...]
    b = frac_col[...]

    def hats(delta, frac):
        return [
            jnp.where(delta == o, 1.0 - frac, 0.0) + jnp.where(delta + 1 == o, frac, 0.0)
            for o in range(-HW, HW + 1)
        ]

    row_hats, col_hats = hats(delta_row, a), hats(delta_col, b)
    weight_ref[...] = jnp.zeros_like(weight_ref)
    for d in range(TAPS):
        for e in range(TAPS):
            weight_ref[d * TAPS + e, :, :cols] = row_hats[d] * col_hats[e]
    taps = [
        pltpu.roll(weight_ref[d * TAPS + e], e, 1) if e else weight_ref[d * TAPS]
        for d in range(TAPS)
        for e in range(TAPS)
    ]
    depth = grid_ref.shape[1]
    for p in range(PEERS):
        buf[p * depth : (p + 1) * depth, :] = grid_ref[p].astype(jnp.float32)

    def body(i, carry):
        p, j = i // J, i % J
        z = p % ZC + ZC * j
        field = ((p // ZC) * ZS + z) * fields
        for f in range(fields):
            base = i * (fields * WIN) + f * WIN
            planes = [buf[pl.ds(base + d, rows), :] for d in range(TAPS)]
            result = None
            for e in range(TAPS):
                column = planes[0] * taps[e]
                for d in range(1, TAPS):
                    column = column + planes[d] * taps[d * TAPS + e]
                column = pltpu.roll(column, LANES - e, 1) if e else column
                result = column if result is None else result + column
            out_ref[field + f] = result[:, :cols]
        return carry

    lax.fori_loop(0, PEERS * J, body, 0)


def exchange_groups(bands):
    first, second = [], []
    for x in range(XS):
        for i in range(ZC):
            first.append(
                [b * XS * ZS + x * ZS + i + ZC * j for b in range(bands) for j in range(J)]
            )
    for b in range(bands):
        shift = ZC // 2 if b % 2 and J > 1 else 0
        for g in range(J):
            window = sorted(((ZC * g + shift + n) % ZS for n in range(ZC)), key=lambda z: z % ZC)
            second.append([b * XS * ZS + x * ZS + z for x in range(XS) for z in window])
    return first, second


def local(spectra, legendre, wavenum, dep_row, dep_col, frac_row, frac_col):
    bands = lax.axis_size("band")
    band = lax.axis_index("band")
    field = lax.axis_index("field")
    slots, parts, fields, degrees = spectra.shape
    lats = legendre.shape[1]
    waves = wavenum.shape[0]
    rows, cols = dep_row.shape
    first, second = exchange_groups(bands)
    vmem = pl.BlockSpec(memory_space=pltpu.VMEM)
    hbm = pl.BlockSpec(memory_space=pltpu.HBM)
    smem = pl.BlockSpec(memory_space=pltpu.SMEM)

    four = pl.pallas_call(
        legendre_kernel,
        out_shape=jax.ShapeDtypeStruct((bands * J, SLAB, LANES), jnp.bfloat16),
        in_specs=[smem, hbm, hbm],
        out_specs=vmem,
        scratch_shapes=[
            pltpu.VMEM(spectra.shape, jnp.bfloat16),
            pltpu.VMEM(legendre.shape, jnp.bfloat16),
            pltpu.VMEM((lats + SLAB, LANES), jnp.float32),
            pltpu.SemaphoreType.DMA,
            pltpu.SemaphoreType.DMA((slots,)),
        ],
        compiler_params=pltpu.CompilerParams(vmem_limit_bytes=24 * MIB),
        cost_estimate=pl.CostEstimate(
            flops=2 * slots * LANES * lats * degrees, bytes_accessed=6 * MIB, transcendentals=0
        ),
        name="legendre",
    )(wavenum, spectra, legendre)
    rows_here = lax.all_to_all(
        four, ("band", "field"), split_axis=0, concat_axis=0, tiled=True, axis_index_groups=first
    )

    z_here = field % ZS
    mod_here = z_here % ZC
    shift = jnp.where(band % 2 == 1, ZC // 2 if J > 1 else 0, 0)
    group = (z_here // ZC - jnp.where(mod_here < shift, 1, 0)) % J
    peer = jnp.minimum(lax.iota(jnp.int32, LANES), PEERS - 1)
    mod_peer = peer % ZC
    z_peer = (ZC * group + mod_peer + jnp.where(mod_peer < shift, ZC, 0)) % ZS
    start = ((peer // ZC) * ZS + z_peer) * cols - HW
    start = jnp.where(start < 0, start + NLON, start)
    wave_rows = jnp.broadcast_to(wavenum[:, None], (waves, parts)).reshape(waves * parts, 1)
    table = pl.pallas_call(
        table_kernel,
        out_shape=jax.ShapeDtypeStruct((waves * parts, PEERS * LANES), jnp.bfloat16),
        in_specs=[vmem, vmem],
        out_specs=vmem,
        compiler_params=pltpu.CompilerParams(vmem_limit_bytes=24 * MIB),
        cost_estimate=pl.CostEstimate(
            flops=20 * MIB, bytes_accessed=4 * MIB, transcendentals=MIB // 4
        ),
        name="table",
    )(wave_rows.astype(jnp.float32), start.astype(jnp.float32)[None, :])

    depth = J * fields * WIN
    grid = pl.pallas_call(
        fourier_kernel,
        out_shape=jax.ShapeDtypeStruct((PEERS, depth, LANES), jnp.bfloat16),
        in_specs=[vmem, vmem],
        out_specs=vmem,
        scratch_shapes=[pltpu.VMEM((depth, waves * parts), jnp.float32)],
        compiler_params=pltpu.CompilerParams(vmem_limit_bytes=24 * MIB),
        cost_estimate=pl.CostEstimate(
            flops=2 * depth * waves * parts * PEERS * LANES,
            bytes_accessed=3 * MIB,
            transcendentals=0,
        ),
        name="fourier",
    )(rows_here, table)
    segment = lax.all_to_all(
        grid, ("band", "field"), split_axis=0, concat_axis=0, tiled=True, axis_index_groups=second
    )
    total_fields = XS * ZS * fields
    return pl.pallas_call(
        interp_kernel,
        out_shape=jax.ShapeDtypeStruct((total_fields, rows, cols), jnp.float32),
        in_specs=[vmem] * 5,
        out_specs=vmem,
        scratch_shapes=[
            pltpu.VMEM((PEERS * depth, LANES), jnp.float32),
            pltpu.VMEM((TAPS * TAPS, rows, LANES), jnp.float32),
        ],
        compiler_params=pltpu.CompilerParams(vmem_limit_bytes=24 * MIB),
        cost_estimate=pl.CostEstimate(
            flops=50 * total_fields * rows * LANES, bytes_accessed=2 * MIB, transcendentals=0
        ),
        name="interp",
    )(segment, dep_row, dep_col, frac_row, frac_col)


def solution(mesh):
    return jax.shard_map(
        local,
        mesh=mesh,
        in_specs=(
            P("band", None, "field", None),
            P("band", None, None),
            P(),
            P("band", "field"),
            P("band", "field"),
            P("band", "field"),
            P("band", "field"),
        ),
        out_specs=P(None, "band", "field"),
        check_vma=False,
    )
```

time: 155 us -> 77.2 us (0.50)
  local copies, waits for them, and re-layouts: 47.4 us -> 4.35 us
  other arithmetic: 32.5 us -> 0.03 us
  blocking collectives: 0 us -> 25 us
  waiting for transfers between devices: 28.3 us -> 9.47 us
  Pallas kernels: 0 us -> 16.9 us
  starting transfers between devices: 33.3 us -> 21.1 us
  matrix products: 11.5 us -> 0 us
    all_to_all x0 -> x1, blocking collectives: none -> 25 us  [local(): lax.all_to_all(grid, ('band', 'field'), split_axis=0, concat_axis=0, tile...]
    another operation x2 -> x0, other arithmetic: 23.5 us -> none
    pallas_call x0 -> x4, Pallas kernels: none -> 16.9 us  [the longest x1 6.57 us: local(): pl.pallas_call(legendre_kernel, out_shape=jax.ShapeDtypeStruct((bands * J...]
    unnamed x14 -> x16, local copies, waits for them, and re-layouts: 19 us -> 4.16 us
    convert_element_type x3 -> x1, local copies, waits for them, and re-layouts: 12.6 us -> 0.11 us  [local(): wave_rows.astype(jnp.float32)]
    ppermute x4 -> x0, waiting for transfers between devices: 11.8 us -> none  [the longest x2 6.79 us: with_halo(): lax.ppermute(lax.slice_in_dim(block, 0, width, axis=dim), axis, backward)]
    dot_general x6 -> x0, matrix products: 11.5 us -> none  [the longest x5 8.28 us: legendre_block(): jnp.einsum('scfj,slj->scfl', spec_part, table_part, preferred_element_typ...]
    ppermute x4 -> x0, starting transfers between devices: 10.2 us -> none  [the longest x2 6.19 us: with_halo(): lax.ppermute(lax.slice_in_dim(block, 0, width, axis=dim), axis, backward)]
  transfers between devices with their start and end apart: 6 -> 1, of which waited for: 4 -> 1; matrix products, arithmetic and copies ran while one was open for 26% -> 0% of each run, Pallas kernels for 0% -> 5%
where the time goes in v1:
time: 77.2 us; the launch traced here: 77 us
  blocking collectives  25 us (32%)
  starting transfers between devices  21.1 us (27%)
  Pallas kernels  16.9 us (22%)
  waiting for transfers between devices  9.47 us (12%)
  local copies, waits for them, and re-layouts  4.35 us (6%)
    all_to_all x1, blocking collectives, local(): lax.all_to_all(grid, ('band', 'field'), split_axis=0, concat_axis=0, tile...  25 us
    all_to_all x1, starting transfers between devices, local(): lax.all_to_all(four, ('band', 'field'), split_axis=0, concat_axis=0, tile...  21.1 us
    all_to_all x1, waiting for transfers between devices, local(): lax.all_to_all(four, ('band', 'field'), split_axis=0, concat_axis=0, tile...  9.47 us
    pallas_call x1, Pallas kernels, local(): pl.pallas_call(legendre_kernel, out_shape=jax.ShapeDtypeStruct((bands * J...  6.57 us
    pallas_call x1, Pallas kernels, local(): pl.pallas_call(interp_kernel, out_shape=jax.ShapeDtypeStruct((total_field...  5.48 us
    pallas_call x1, Pallas kernels, local(): pl.pallas_call(table_kernel, out_shape=jax.ShapeDtypeStruct((waves * part...  4.2 us
    unnamed x16, local copies, waits for them, and re-layouts  4.16 us
  transfers between devices with their start and end apart: 1, of which 1 were waited for; matrix products, arithmetic and copies ran while one was open for 0% of the time, Pallas kernels for 5%

profile of v1, /device:TPU:1, one launch (start us, length us, event | category | flops | bytes accessed | tf_op | source)
XLA Modules:
  0.0 77.0 jit_solution(4728051949312922920)
XLA Ops:
  0.0 0.0 copy-start
  0.0 2.5 %copy-done = bf16[16,128,1280]{2,1,0:T(8,128)(2,1)S(1)} copy-done((bf16[16,128,1280]{2,1,0:T(8,128)(2,1)S(1)}, bf16[16,128,1280]{2,1,0:T(8,128)(2,1)}, u32[]{:S(2)}) %copy-start) | copy-done | bytes 5242904
  2.5 0.0 copy-start.1
  2.5 1.0 %copy-done.1 = bf16[16,2,4,1280]{3,2,1,0:T(4,128)(2,1)S(1)} copy-done((bf16[16,2,4,1280]{3,2,1,0:T(4,128)(2,1)S(1)}, bf16[16,2,4,1280]{3,2,1,0:T(4,128)(2,1)}, u32[]{:S(2)}) %copy-start.1) | copy-done | bytes 327704
  3.5 0.0 copy-start.6
  3.5 0.7 copy-done.6
  4.1 0.0 copy-start.7
  4.1 0.0 copy-start.2
  4.1 0.0 copy-start.3
  4.1 0.0 copy-start.4
  4.2 0.0 copy-start.5
  4.2 6.6 %legendre.1 = bf16[48,16,128]{2,1,0:T(8,128)(2,1)} custom-call(s32[256]{0:T(256)S(1)} %copy-done.6, bf16[16,2,4,1280]{3,2,1,0:T(4,128)(2,1)S(1)} %copy-done.1, bf16[16,128,1280]{2,1,0:T(8,128)(2,1)S(1)} %copy-done), custom_call_target="tpu_custom_call" | custom-call | flops 671088640 | bytes 6291456 | tf_op jit(solution)/shard_map/legendre/pallas_call | solution.py:199
  10.7 21.1 %all-to-all-start = ((bf16[48,16,128]{2,1,0:T(8,128)(2,1)}), bf16[48,16,128]{2,1,0:T(8,128)(2,1)S(1)}, u32[]{:S(2)}, u32[]{:S(2)}) async-start(bf16[48,16,128]{2,1,0:T(8,128)(2,1)} %legendre.1), calls=%async_computation | async-start | bytes 393216 | tf_op jit(solution)/shard_map/all_to_all | solution.py:217
  31.9 0.0 copy-done.7
  31.9 0.1 broadcast_in_dim.6
  32.0 0.1 convert_element_type.18.wave_ref
  32.2 4.2 %table.1.table_ref = bf16[512,2048]{1,0:T(8,128)(2,1)S(1)} custom-call(f32[512,1]{1,0:T(8,128)S(1)} %convert_element_type.18.wave_ref, f32[1,128]{1,0:T(1,128)S(1)} %fusion.2.start_ref), custom_call_target="tpu_custom_call" | custom-call | flops 20971520 | bytes 4194304 | tf_op jit(solution)/shard_map/table/pallas_call | solution.py:231
  36.4 9.5 %all-to-all-done.four_ref = bf16[48,16,128]{2,1,0:T(8,128)(2,1)S(1)} async-done(((bf16[48,16,128]{2,1,0:T(8,128)(2,1)}), bf16[48,16,128]{2,1,0:T(8,128)(2,1)S(1)}, u32[]{:S(2)}, u32[]{:S(2)}) %all-to-all-start) | async-done | bytes 196640 | tf_op jit(solution)/shard_map/all_to_all | solution.py:217
  45.8 0.6 fourier.1
  46.5 25.0 %all_to_all.10.grid_ref = bf16[16,144,128]{2,1,0:T(8,128)(2,1)S(1)} all-to-all(bf16[16,144,128]{2,1,0:T(8,128)(2,1)S(1)} %fourier.1), channel_id=1, replica_groups={{0,1,2,3,12,13,14,15,24,25,26,27,36,37,38,39},{4,5,6,7,16,17,18,19,28,2..., dimensions={0} | all-to-all | bytes 1179648 | tf_op jit(solution)/shard_map/all_to_all | solution.py:258
  71.5 0.0 copy-done.2
  71.5 0.0 copy-done.3
  71.5 0.0 copy-done.4
  71.5 0.0 copy-done.5
  71.5 5.5 %interp.1 = f32[192,8,96]{2,1,0:T(8,128)} custom-call(bf16[16,144,128]{2,1,0:T(8,128)(2,1)S(1)} %all_to_all.10.grid_ref, s32[8,96]{1,0:T(8,128)S(1)} %copy-done.2, s32[8,96]{1,0:T(8,128)S(1)} %copy-done.3, f32[8,96]{1,0:T(8,128)S(1)} %copy-done.4, f32[8,96]{1,0:T(8,128)S(1)} %copy-done.5), custom_call_target="tpu_custom_call" | custom-call | flops 9830400 | bytes 2097152 | tf_op jit(solution)/shard_map/interp/pallas_call | solution.py:262
  (2 shorter events, 0.0 us)
Async XLA Ops:
  0.0 2.5 %copy-start = (bf16[16,128,1280]{2,1,0:T(8,128)(2,1)S(1)}, bf16[16,128,1280]{2,1,0:T(8,128)(2,1)}, u32[]{:S(2)}) copy-start(bf16[16,128,1280]{2,1,0:T(8,128)(2,1)} %leg_hbm.1) | copy-start | bytes 15728644
  2.5 1.0 %copy-start.1 = (bf16[16,2,4,1280]{3,2,1,0:T(4,128)(2,1)S(1)}, bf16[16,2,4,1280]{3,2,1,0:T(4,128)(2,1)}, u32[]{:S(2)}) copy-start(bf16[16,2,4,1280]{3,2,1,0:T(4,128)(2,1)} %spec_hbm.1) | copy-start | bytes 983044
  3.5 0.7 copy-start.6
  4.1 27.8 %copy-start.7 = (s32[256]{0:T(256)S(1)}, s32[256]{0:T(256)}, u32[]{:S(2)}) copy-start(s32[256]{0:T(256)} %wave_ref.1) | copy-start | bytes 3076
  4.1 67.3 %copy-start.2 = (s32[8,96]{1,0:T(8,128)S(1)}, s32[8,96]{1,0:T(8,128)}, u32[]{:S(2)}) copy-start(s32[8,96]{1,0:T(8,128)} %dep_row.1) | copy-start | bytes 9220
  4.1 67.3 %copy-start.3 = (s32[8,96]{1,0:T(8,128)S(1)}, s32[8,96]{1,0:T(8,128)}, u32[]{:S(2)}) copy-start(s32[8,96]{1,0:T(8,128)} %dep_col.1) | copy-start | bytes 9220
  4.1 67.3 %copy-start.4 = (f32[8,96]{1,0:T(8,128)S(1)}, f32[8,96]{1,0:T(8,128)}, u32[]{:S(2)}) copy-start(f32[8,96]{1,0:T(8,128)} %frac_row.1) | copy-start | bytes 9220
  4.2 67.3 %copy-start.5 = (f32[8,96]{1,0:T(8,128)S(1)}, f32[8,96]{1,0:T(8,128)}, u32[]{:S(2)}) copy-start(f32[8,96]{1,0:T(8,128)} %frac_col.1) | copy-start | bytes 9220
  10.7 35.1 %all-to-all-start = ((bf16[48,16,128]{2,1,0:T(8,128)(2,1)}), bf16[48,16,128]{2,1,0:T(8,128)(2,1)S(1)}, u32[]{:S(2)}, u32[]{:S(2)}) async-start(bf16[48,16,128]{2,1,0:T(8,128)(2,1)} %legendre.1), calls=%async_computation | async-start | bytes 393216 | tf_op jit(solution)/shard_map/all_to_all | solution.py:217

commit v2 on v1

--- a/solution.py
+++ b/solution.py
@@ -15,50 +15,58 @@
 TAPS = 2 * HW + 1
 WIN = 12
 SLAB = 16
+CHUNKS = 1
 LANES = 128
 MIB = 1024 * 1024
 
 
-def legendre_kernel(wave_ref, spec_hbm, leg_hbm, out_ref, spec_buf, leg_buf, pad_ref, spec_sem, leg_sem):
+def legendre_kernel(
+    wave_hbm, spec_hbm, leg_hbm, out_ref, wave_ref, spec_buf, leg_buf, pad_ref, small_sem, leg_sem
+):
     slots, parts, fields, degrees = spec_buf.shape
     lats = leg_buf.shape[1]
     group = parts * fields
-    spec_copy = pltpu.make_async_copy(spec_hbm, spec_buf, spec_sem)
+    chunks = leg_sem.shape[0]
+    per_chunk = slots // chunks
+    wave_copy = pltpu.make_async_copy(wave_hbm, wave_ref, small_sem.at[0])
+    spec_copy = pltpu.make_async_copy(spec_hbm, spec_buf, small_sem.at[1])
     spec_copy.start()
-    leg_copies = [
-        pltpu.make_async_copy(leg_hbm.at[s], leg_buf.at[s], leg_sem.at[s]) for s in range(slots)
-    ]
+    wave_copy.start()
+    leg_copies = []
+    for c in range(chunks):
+        part = pl.ds(c * per_chunk, per_chunk)
+        leg_copies.append(
+            pltpu.make_async_copy(leg_hbm.at[part], leg_buf.at[part], leg_sem.at[c])
+        )
     for copy in leg_copies:
         copy.start()
     first = lax.axis_index("band") * slots
-    pad_ref[...] = jnp.zeros_like(pad_ref)
+    pad_ref[:8, :] = jnp.zeros((8, LANES), jnp.float32)
+    pad_ref[lats:, :] = jnp.zeros((SLAB, LANES), jnp.float32)
     lane_in = lax.broadcasted_iota(jnp.int32, (LANES, LANES), 0)
     lane_out = lax.broadcasted_iota(jnp.int32, (LANES, LANES), 1)
     order = (lane_in % fields) * (LANES // fields) + lane_in // fields
     perm = jnp.where(order == lane_out, 1.0, 0.0).astype(jnp.bfloat16)
     position = lax.broadcasted_iota(jnp.int32, (group, degrees), 1)
-    zeros8 = jnp.zeros((group, degrees), jnp.float32)
+    slot_of_lane = lax.broadcasted_iota(jnp.int32, (lats, LANES), 1) // group
+    wave_copy.wait()
     spec_copy.wait()
-    total = jnp.zeros((lats, LANES), jnp.float32)
+    kept = []
     for s in range(slots):
         part = spec_buf[s].astype(jnp.float32)
         rows = jnp.concatenate([part[0], part[1]], axis=0)
-        rows = jnp.where(position < degrees - wave_ref[first + s], rows, 0.0)
-        pair = [rows, zeros8] if s % 2 == 0 else [zeros8, rows]
-        tile = jnp.concatenate(pair, axis=0).astype(jnp.bfloat16)
-        pieces = []
-        if s // 2 > 0:
-            pieces.append(jnp.zeros((2 * group * (s // 2), degrees), jnp.bfloat16))
-        pieces.append(tile)
-        if s // 2 < slots // 2 - 1:
-            pieces.append(
-                jnp.zeros((2 * group * (slots // 2 - 1 - s // 2), degrees), jnp.bfloat16)
-            )
-        weights = jnp.concatenate(pieces, axis=0)
-        leg_copies[s].wait()
-        total = total + lax.dot_general(
-            leg_buf[s], weights, (((1,), (1,)), ((), ())), preferred_element_type=jnp.float32
+        kept.append(jnp.where(position < degrees - wave_ref[first + s], rows, 0.0))
+    weights = jnp.concatenate(kept, axis=0).astype(jnp.bfloat16)
+    total = jnp.zeros((lats, LANES), jnp.float32)
+    for c in range(chunks):
+        leg_copies[c].wait()
+        rows = leg_buf[c * per_chunk : (c + 1) * per_chunk].reshape(per_chunk * lats, degrees)
+        products = lax.dot_general(
+            rows, weights, (((1,), (1,)), ((), ())), preferred_element_type=jnp.float32
         )
+        for n in range(per_chunk):
+            own = slot_of_lane == c * per_chunk + n
+            total = jnp.where(own, products[n * lats : (n + 1) * lats], total)
     four = jnp.dot(total.astype(jnp.bfloat16), perm, preferred_element_type=jnp.float32)
     pad_ref[HW : HW + lats, :] = four
     bands = out_ref.shape[0] // J
@@ -148,12 +156,9 @@
     for p in range(PEERS):
         buf[p * depth : (p + 1) * depth, :] = grid_ref[p].astype(jnp.float32)
 
-    def body(i, carry):
-        p, j = i // J, i % J
-        z = p % ZC + ZC * j
-        field = ((p // ZC) * ZS + z) * fields
-        for f in range(fields):
-            base = i * (fields * WIN) + f * WIN
+    def body(p, carry):
+        for t in range(J * fields):
+            base = pl.multiple_of(p * depth, 8) + t * WIN
             planes = [buf[pl.ds(base + d, rows), :] for d in range(TAPS)]
             result = None
             for e in range(TAPS):
@@ -162,10 +167,11 @@
                     column = column + planes[d] * taps[d * TAPS + e]
                 column = pltpu.roll(column, LANES - e, 1) if e else column
                 result = column if result is None else result + column
-            out_ref[field + f] = result[:, :cols]
+            z = p // XS + ZC * (t // fields)
+            out_ref[((p % XS) * ZS + z) * fields + t % fields] = result[:, :cols]
         return carry
 
-    lax.fori_loop(0, PEERS * J, body, 0)
+    lax.fori_loop(0, PEERS, body, 0)
 
 
 def exchange_groups(bands):
@@ -179,7 +185,7 @@
         shift = ZC // 2 if b % 2 and J > 1 else 0
         for g in range(J):
             window = sorted(((ZC * g + shift + n) % ZS for n in range(ZC)), key=lambda z: z % ZC)
-            second.append([b * XS * ZS + x * ZS + z for x in range(XS) for z in window])
+            second.append([b * XS * ZS + x * ZS + z for z in window for x in range(XS)])
     return first, second
 
 
@@ -194,21 +200,21 @@
     first, second = exchange_groups(bands)
     vmem = pl.BlockSpec(memory_space=pltpu.VMEM)
     hbm = pl.BlockSpec(memory_space=pltpu.HBM)
-    smem = pl.BlockSpec(memory_space=pltpu.SMEM)
 
     four = pl.pallas_call(
         legendre_kernel,
         out_shape=jax.ShapeDtypeStruct((bands * J, SLAB, LANES), jnp.bfloat16),
-        in_specs=[smem, hbm, hbm],
+        in_specs=[hbm, hbm, hbm],
         out_specs=vmem,
         scratch_shapes=[
+            pltpu.SMEM(wavenum.shape, jnp.int32),
             pltpu.VMEM(spectra.shape, jnp.bfloat16),
             pltpu.VMEM(legendre.shape, jnp.bfloat16),
             pltpu.VMEM((lats + SLAB, LANES), jnp.float32),
-            pltpu.SemaphoreType.DMA,
-            pltpu.SemaphoreType.DMA((slots,)),
+            pltpu.SemaphoreType.DMA((2,)),
+            pltpu.SemaphoreType.DMA((CHUNKS,)),
         ],
-        compiler_params=pltpu.CompilerParams(vmem_limit_bytes=24 * MIB),
+        compiler_params=pltpu.CompilerParams(vmem_limit_bytes=60 * MIB),
         cost_estimate=pl.CostEstimate(
             flops=2 * slots * LANES * lats * degrees, bytes_accessed=6 * MIB, transcendentals=0
         ),
@@ -223,9 +229,9 @@
     shift = jnp.where(band % 2 == 1, ZC // 2 if J > 1 else 0, 0)
     group = (z_here // ZC - jnp.where(mod_here < shift, 1, 0)) % J
     peer = jnp.minimum(lax.iota(jnp.int32, LANES), PEERS - 1)
-    mod_peer = peer % ZC
+    mod_peer = peer // XS
     z_peer = (ZC * group + mod_peer + jnp.where(mod_peer < shift, ZC, 0)) % ZS
-    start = ((peer // ZC) * ZS + z_peer) * cols - HW
+    start = ((peer % XS) * ZS + z_peer) * cols - HW
     start = jnp.where(start < 0, start + NLON, start)
     wave_rows = jnp.broadcast_to(wavenum[:, None], (waves, parts)).reshape(waves * parts, 1)
     table = pl.pallas_call(

time: 77.2 us -> 69 us (0.89)
  local copies, waits for them, and re-layouts: 4.35 us -> 0.21 us
  Pallas kernels: 16.9 us -> 13 us
    unnamed x16 -> x10, local copies, waits for them, and re-layouts: 4.16 us -> 0.02 us
    pallas_call x1, Pallas kernels: 5.48 us -> 3.17 us  [local(): pl.pallas_call(interp_kernel, out_shape=jax.ShapeDtypeStruct((total_field...]
    pallas_call x1, Pallas kernels: 6.57 us -> 4.99 us  [local(): pl.pallas_call(legendre_kernel, out_shape=jax.ShapeDtypeStruct((bands * J...]
  transfers between devices with their start and end apart: 1 -> 1, of which waited for: 1 -> 1; matrix products, arithmetic and copies ran while one was open for 0% -> 0% of each run, Pallas kernels for 5% -> 6%
where the time goes in v2:
time: 69 us; the launch traced here: 68.8 us
  blocking collectives  24.8 us (36%)
  starting transfers between devices  21.1 us (31%)
  Pallas kernels  13 us (19%)
  waiting for transfers between devices  9.47 us (14%)
    all_to_all x1, blocking collectives, local(): lax.all_to_all(grid, ('band', 'field'), split_axis=0, concat_axis=0, tile...  24.8 us
    all_to_all x1, starting transfers between devices, local(): lax.all_to_all(four, ('band', 'field'), split_axis=0, concat_axis=0, tile...  21.1 us
    all_to_all x1, waiting for transfers between devices, local(): lax.all_to_all(four, ('band', 'field'), split_axis=0, concat_axis=0, tile...  9.47 us
    pallas_call x1, Pallas kernels, local(): pl.pallas_call(legendre_kernel, out_shape=jax.ShapeDtypeStruct((bands * J...  4.99 us
    pallas_call x1, Pallas kernels, local(): pl.pallas_call(table_kernel, out_shape=jax.ShapeDtypeStruct((waves * part...  4.2 us
    pallas_call x1, Pallas kernels, local(): pl.pallas_call(interp_kernel, out_shape=jax.ShapeDtypeStruct((total_field...  3.17 us
  transfers between devices with their start and end apart: 1, of which 1 were waited for; matrix products, arithmetic and copies ran while one was open for 0% of the time, Pallas kernels for 6%

profile of v2, /device:TPU:1, one launch (start us, length us, event | category | flops | bytes accessed | tf_op | source)
XLA Modules:
  0.0 68.8 jit_solution(14481892360492057293)
XLA Ops:
  0.0 0.0 copy-start.4
  0.0 0.0 copy-start.3
  0.0 0.0 copy-start.2
  0.0 0.0 copy-start.1
  0.0 0.0 copy-start
  0.0 5.0 %legendre.1 = bf16[48,16,128]{2,1,0:T(8,128)(2,1)} custom-call(s32[256]{0:T(256)} %wave_hbm.1, bf16[16,2,4,1280]{3,2,1,0:T(4,128)(2,1)} %spec_hbm.1, bf16[16,128,1280]{2,1,0:T(8,128)(2,1)} %leg_hbm.1), custom_call_target="tpu_custom_call" | custom-call | flops 671088640 | bytes 6291456 | tf_op jit(solution)/shard_map/legendre/pallas_call | solution.py:204
  5.0 21.1 %all-to-all-start = ((bf16[48,16,128]{2,1,0:T(8,128)(2,1)}), bf16[48,16,128]{2,1,0:T(8,128)(2,1)S(1)}, u32[]{:S(2)}, u32[]{:S(2)}) async-start(bf16[48,16,128]{2,1,0:T(8,128)(2,1)} %legendre.1), calls=%async_computation | async-start | bytes 393216 | tf_op jit(solution)/shard_map/all_to_all | solution.py:223
  26.2 0.0 copy-done.4
  26.2 0.1 broadcast_in_dim.6
  26.3 0.1 convert_element_type.18.wave_ref
  26.5 4.2 %table.1.table_ref = bf16[512,2048]{1,0:T(8,128)(2,1)S(1)} custom-call(f32[512,1]{1,0:T(8,128)S(1)} %convert_element_type.18.wave_ref, f32[1,128]{1,0:T(1,128)S(1)} %fusion.3.start_ref), custom_call_target="tpu_custom_call" | custom-call | flops 20971520 | bytes 4194304 | tf_op jit(solution)/shard_map/table/pallas_call | solution.py:237
  30.7 9.5 %all-to-all-done.four_ref = bf16[48,16,128]{2,1,0:T(8,128)(2,1)S(1)} async-done(((bf16[48,16,128]{2,1,0:T(8,128)(2,1)}), bf16[48,16,128]{2,1,0:T(8,128)(2,1)S(1)}, u32[]{:S(2)}, u32[]{:S(2)}) %all-to-all-start) | async-done | bytes 196640 | tf_op jit(solution)/shard_map/all_to_all | solution.py:223
  40.1 0.6 fourier.1
  40.8 24.8 %all_to_all.10.grid_ref = bf16[16,144,128]{2,1,0:T(8,128)(2,1)S(1)} all-to-all(bf16[16,144,128]{2,1,0:T(8,128)(2,1)S(1)} %fourier.1), channel_id=1, replica_groups={{0,12,24,36,1,13,25,37,2,14,26,38,3,15,27,39},{4,16,28,40,5,17,29,41,6,..., dimensions={0} | all-to-all | bytes 1179648 | tf_op jit(solution)/shard_map/all_to_all | solution.py:264
  65.6 0.0 copy-done.3
  65.6 0.0 copy-done.2
  65.6 0.0 copy-done.1
  65.6 0.0 copy-done
  65.6 3.2 %interp.1 = f32[192,8,96]{2,1,0:T(8,128)} custom-call(bf16[16,144,128]{2,1,0:T(8,128)(2,1)S(1)} %all_to_all.10.grid_ref, s32[8,96]{1,0:T(8,128)S(1)} %copy-done, s32[8,96]{1,0:T(8,128)S(1)} %copy-done.1, f32[8,96]{1,0:T(8,128)S(1)} %copy-done.2, f32[8,96]{1,0:T(8,128)S(1)} %copy-done.3), custom_call_target="tpu_custom_call" | custom-call | flops 9830400 | bytes 2097152 | tf_op jit(solution)/shard_map/interp/pallas_call | solution.py:268
  (2 shorter events, 0.0 us)
Async XLA Ops:
  0.0 26.2 %copy-start.4 = (s32[256]{0:T(256)S(1)}, s32[256]{0:T(256)}, u32[]{:S(2)}) copy-start(s32[256]{0:T(256)} %wave_hbm.1) | copy-start | bytes 3076
  0.0 65.6 %copy-start.3 = (f32[8,96]{1,0:T(8,128)S(1)}, f32[8,96]{1,0:T(8,128)}, u32[]{:S(2)}) copy-start(f32[8,96]{1,0:T(8,128)} %frac_col.1) | copy-start | bytes 9220
  0.0 65.6 %copy-start.2 = (f32[8,96]{1,0:T(8,128)S(1)}, f32[8,96]{1,0:T(8,128)}, u32[]{:S(2)}) copy-start(f32[8,96]{1,0:T(8,128)} %frac_row.1) | copy-start | bytes 9220
  0.0 65.6 %copy-start.1 = (s32[8,96]{1,0:T(8,128)S(1)}, s32[8,96]{1,0:T(8,128)}, u32[]{:S(2)}) copy-start(s32[8,96]{1,0:T(8,128)} %dep_col.1) | copy-start | bytes 9220
  0.0 65.6 %copy-start = (s32[8,96]{1,0:T(8,128)S(1)}, s32[8,96]{1,0:T(8,128)}, u32[]{:S(2)}) copy-start(s32[8,96]{1,0:T(8,128)} %dep_row.1) | copy-start | bytes 9220
  5.0 35.1 %all-to-all-start = ((bf16[48,16,128]{2,1,0:T(8,128)(2,1)}), bf16[48,16,128]{2,1,0:T(8,128)(2,1)S(1)}, u32[]{:S(2)}, u32[]{:S(2)}) async-start(bf16[48,16,128]{2,1,0:T(8,128)(2,1)} %legendre.1), calls=%async_computation | async-start | bytes 393216 | tf_op jit(solution)/shard_map/all_to_all | solution.py:223

commit v3 on v2

--- a/solution.py
+++ b/solution.py
@@ -16,6 +16,9 @@
 WIN = 12
 SLAB = 16
 CHUNKS = 1
+WIDE = 64
+SPLIT = WIDE - 2 * HW
+THIN = 40
 LANES = 128
 MIB = 1024 * 1024
 
@@ -76,25 +79,41 @@
             out_ref[b * J + j] = tile
 
 
-def reduced_angle(product):
-    turns = jnp.floor(product * (1.0 / NLON))
-    return (product - turns * NLON) * (2.0 * 3.141592653589793 / NLON)
+def turn_parts(product):
+    quarters = product * (4.0 / NLON)
+    nearest = jnp.floor(quarters + 0.5)
+    x = (product - nearest * (NLON / 4)) * (2.0 * 3.141592653589793 / NLON)
+    square = x * x
+    sine = x * (1.0 + square * (-1.0 / 6 + square * (1.0 / 120 + square * (-1.0 / 5040 + square * (1.0 / 362880)))))
+    cosine = 1.0 + square * (
+        -0.5 + square * (1.0 / 24 + square * (-1.0 / 720 + square * (1.0 / 40320 - square * (1.0 / 3628800))))
+    )
+    quadrant = nearest.astype(jnp.int32)
+    swap = (quadrant & 1) == 1
+    cos_value = jnp.where(swap, sine, cosine)
+    sin_value = jnp.where(swap, cosine, sine)
+    cos_value = jnp.where(((quadrant + 1) & 2) == 2, -cos_value, cos_value)
+    sin_value = jnp.where((quadrant & 2) == 2, -sin_value, sin_value)
+    return cos_value, sin_value
 
 
 def table_kernel(wave_ref, start_ref, out_ref):
     rows = out_ref.shape[0]
     wave = wave_ref[...]
-    lane = lax.broadcasted_iota(jnp.int32, (rows, LANES), 1).astype(jnp.float32)
+    lane = lax.broadcasted_iota(jnp.int32, (rows, LANES), 1)
     part = (lax.broadcasted_iota(jnp.int32, (rows, LANES), 0) % 2).astype(jnp.float32)
     weight = jnp.where(wave == 0.0, 1.0, 2.0)
-    inner = reduced_angle(wave * lane)
-    outer = reduced_angle(wave * start_ref[...] + part * (NLON // 4))
-    cos_in, sin_in = jnp.cos(inner), jnp.sin(inner)
-    cos_out, sin_out = weight * jnp.cos(outer), weight * jnp.sin(outer)
+    column_a = lane & (WIDE - 1)
+    column_b = jnp.where(lane < THIN, lane, jnp.where(lane < 2 * THIN, lane - THIN, lane - 2 * THIN))
+    column_b = column_b + SPLIT
+    inner = [turn_parts(wave * column.astype(jnp.float32)) for column in (column_a, column_b)]
+    cos_out, sin_out = turn_parts(wave * start_ref[...] + part * (NLON // 4))
+    cos_out, sin_out = weight * cos_out, weight * sin_out
     for p in range(PEERS):
-        out_ref[:, p * LANES : (p + 1) * LANES] = (
-            cos_out[:, p : p + 1] * cos_in - sin_out[:, p : p + 1] * sin_in
-        ).astype(jnp.bfloat16)
+        cos_p, sin_p = cos_out[:, p : p + 1], sin_out[:, p : p + 1]
+        for n, (cos_in, sin_in) in enumerate(inner):
+            first = (2 * p + n) * LANES
+            out_ref[:, first : first + LANES] = (cos_p * cos_in - sin_p * sin_in).astype(jnp.bfloat16)
 
 
 def fourier_kernel(four_ref, table_ref, out_ref, flat_ref):
@@ -114,14 +133,24 @@
                 row = (j * fields + f) * WIN
                 flat_ref[row : row + WIN, q * LANES : (q + 1) * LANES] = piece
     flat = flat_ref[...].astype(jnp.bfloat16)
-    for n in range(PEERS // 2):
-        grid = jnp.dot(
+    depth = flat.shape[0]
+    half, third = depth // 2, depth // 3
+    in_low = lax.broadcasted_iota(jnp.int32, (half, LANES), 1) < WIDE
+    lane = lax.broadcasted_iota(jnp.int32, (third, LANES), 1)
+    for p in range(PEERS):
+        both = jnp.dot(
             flat,
-            table_ref[:, 2 * n * LANES : 2 * (n + 1) * LANES],
+            table_ref[:, 2 * p * LANES : 2 * (p + 1) * LANES],
             preferred_element_type=jnp.float32,
-        ).astype(jnp.bfloat16)
-        out_ref[2 * n] = grid[:, :LANES]
-        out_ref[2 * n + 1] = grid[:, LANES:]
+        )
+        wide, thin = both[:, :LANES], both[:, LANES:]
+        wide = jnp.where(in_low, wide[:half], wide[half:])
+        thin = jnp.where(
+            lane < THIN,
+            thin[:third],
+            jnp.where(lane < 2 * THIN, thin[third : 2 * third], thin[2 * third :]),
+        )
+        out_ref[p] = jnp.concatenate([wide, thin], axis=0).astype(jnp.bfloat16)
 
 
 def interp_kernel(grid_ref, dep_row, dep_col, frac_row, frac_col, out_ref, buf, weight_ref):
@@ -143,32 +172,48 @@
         ]
 
     row_hats, col_hats = hats(delta_row, a), hats(delta_col, b)
-    weight_ref[...] = jnp.zeros_like(weight_ref)
+    scratch = weight_ref.shape[0] - 1
+    weight_ref[scratch] = jnp.zeros((rows, LANES), jnp.float32)
+    lane = lax.broadcasted_iota(jnp.int32, (rows, LANES), 1)
     for d in range(TAPS):
         for e in range(TAPS):
-            weight_ref[d * TAPS + e, :, :cols] = row_hats[d] * col_hats[e]
-    taps = [
-        pltpu.roll(weight_ref[d * TAPS + e], e, 1) if e else weight_ref[d * TAPS]
-        for d in range(TAPS)
-        for e in range(TAPS)
-    ]
+            weight_ref[scratch, :, :cols] = row_hats[d] * col_hats[e]
+            tap = weight_ref[scratch]
+            wide = jnp.where(lane < SPLIT, tap, 0.0)
+            thin = pltpu.roll(jnp.where(lane < SPLIT, 0.0, tap), LANES - SPLIT, 1)
+            wide = wide + pltpu.roll(wide, WIDE, 1)
+            thin = thin + pltpu.roll(thin, THIN, 1) + pltpu.roll(thin, 2 * THIN, 1)
+            weight_ref[d * TAPS + e] = pltpu.roll(wide, e, 1) if e else wide
+            weight_ref[TAPS * TAPS + d * TAPS + e] = pltpu.roll(thin, e, 1) if e else thin
     depth = grid_ref.shape[1]
+    per_peer = J * fields
     for p in range(PEERS):
         buf[p * depth : (p + 1) * depth, :] = grid_ref[p].astype(jnp.float32)
 
+    def stencil(base, first_tap):
+        planes = [buf[pl.ds(base + d, rows), :] for d in range(TAPS)]
+        result = None
+        for e in range(TAPS):
+            column = planes[0] * weight_ref[first_tap + e]
+            for d in range(1, TAPS):
+                column = column + planes[d] * weight_ref[first_tap + d * TAPS + e]
+            column = pltpu.roll(column, LANES - e, 1) if e else column
+            result = column if result is None else result + column
+        return result
+
     def body(p, carry):
-        for t in range(J * fields):
-            base = pl.multiple_of(p * depth, 8) + t * WIN
-            planes = [buf[pl.ds(base + d, rows), :] for d in range(TAPS)]
-            result = None
-            for e in range(TAPS):
-                column = planes[0] * taps[e]
-                for d in range(1, TAPS):
-                    column = column + planes[d] * taps[d * TAPS + e]
-                column = pltpu.roll(column, LANES - e, 1) if e else column
-                result = column if result is None else result + column
+        base = pl.multiple_of(p * depth, 8)
+        wide = [stencil(base + u * WIN, 0) for u in range(per_peer // 2)]
+        low = base + (per_peer // 2) * WIN
+        thin = [stencil(low + v * WIN, TAPS * TAPS) for v in range(per_peer // 3)]
+        for t in range(per_peer):
+            left = wide[t % (per_peer // 2)]
+            left = pltpu.roll(left, WIDE, 1) if t >= per_peer // 2 else left
+            right = thin[t % (per_peer // 3)]
+            right = pltpu.roll(right, (SPLIT - THIN * (t // (per_peer // 3))) % LANES, 1)
             z = p // XS + ZC * (t // fields)
-            out_ref[((p % XS) * ZS + z) * fields + t % fields] = result[:, :cols]
+            row = ((p % XS) * ZS + z) * fields + t % fields
+            out_ref[row] = jnp.where(lane < SPLIT, left, right)[:, :cols]
         return carry
 
     lax.fori_loop(0, PEERS, body, 0)
@@ -236,7 +281,7 @@
     wave_rows = jnp.broadcast_to(wavenum[:, None], (waves, parts)).reshape(waves * parts, 1)
     table = pl.pallas_call(
         table_kernel,
-        out_shape=jax.ShapeDtypeStruct((waves * parts, PEERS * LANES), jnp.bfloat16),
+        out_shape=jax.ShapeDtypeStruct((waves * parts, 2 * PEERS * LANES), jnp.bfloat16),
         in_specs=[vmem, vmem],
         out_specs=vmem,
         compiler_params=pltpu.CompilerParams(vmem_limit_bytes=24 * MIB),
@@ -247,9 +292,10 @@
     )(wave_rows.astype(jnp.float32), start.astype(jnp.float32)[None, :])
 
     depth = J * fields * WIN
+    packed = depth // 2 + depth // 3
     grid = pl.pallas_call(
         fourier_kernel,
-        out_shape=jax.ShapeDtypeStruct((PEERS, depth, LANES), jnp.bfloat16),
+        out_shape=jax.ShapeDtypeStruct((PEERS, packed, LANES), jnp.bfloat16),
         in_specs=[vmem, vmem],
         out_specs=vmem,
         scratch_shapes=[pltpu.VMEM((depth, waves * parts), jnp.float32)],
@@ -271,8 +317,8 @@
         in_specs=[vmem] * 5,
         out_specs=vmem,
         scratch_shapes=[
-            pltpu.VMEM((PEERS * depth, LANES), jnp.float32),
-            pltpu.VMEM((TAPS * TAPS, rows, LANES), jnp.float32),
+            pltpu.VMEM((PEERS * packed, LANES), jnp.float32),
+            pltpu.VMEM((2 * TAPS * TAPS + 1, rows, LANES), jnp.float32),
         ],
         compiler_params=pltpu.CompilerParams(vmem_limit_bytes=24 * MIB),
         cost_estimate=pl.CostEstimate(

time: 69 us -> 70.5 us (1.022)
  local copies, waits for them, and re-layouts: 0.21 us -> 4.34 us
  blocking collectives: 24.8 us -> 22.4 us
  waiting for transfers between devices: 9.47 us -> 8.24 us
  Pallas kernels: 13 us -> 14 us
    unnamed x10 -> x14, local copies, waits for them, and re-layouts: 0.02 us -> 4.15 us
    all_to_all x1, blocking collectives: 24.8 us -> 22.4 us  [local(): lax.all_to_all(grid, ('band', 'field'), split_axis=0, concat_axis=0, tile...]
    pallas_call x1, Pallas kernels: 3.17 us -> 4.67 us  [local(): pl.pallas_call(interp_kernel, out_shape=jax.ShapeDtypeStruct((total_field...]
    all_to_all x1, waiting for transfers between devices: 9.47 us -> 8.24 us  [local(): lax.all_to_all(four, ('band', 'field'), split_axis=0, concat_axis=0, tile...]
    pallas_call x1, Pallas kernels: 4.2 us -> 3.44 us  [local(): pl.pallas_call(table_kernel, out_shape=jax.ShapeDtypeStruct((waves * part...]
  transfers between devices with their start and end apart: 1 -> 1, of which waited for: 1 -> 1; matrix products, arithmetic and copies ran while one was open for 0% -> 0% of each run, Pallas kernels for 6% -> 5%
where the time goes in v3:
time: 70.5 us; the launch traced here: 70.3 us
  blocking collectives  22.4 us (32%)
  starting transfers between devices  21.1 us (30%)
  Pallas kernels  14 us (20%)
  waiting for transfers between devices  8.24 us (12%)
  local copies, waits for them, and re-layouts  4.34 us (6%)
    all_to_all x1, blocking collectives, local(): lax.all_to_all(grid, ('band', 'field'), split_axis=0, concat_axis=0, tile...  22.4 us
    all_to_all x1, starting transfers between devices, local(): lax.all_to_all(four, ('band', 'field'), split_axis=0, concat_axis=0, tile...  21.1 us
    all_to_all x1, waiting for transfers between devices, local(): lax.all_to_all(four, ('band', 'field'), split_axis=0, concat_axis=0, tile...  8.24 us
    pallas_call x1, Pallas kernels, local(): pl.pallas_call(legendre_kernel, out_shape=jax.ShapeDtypeStruct((bands * J...  4.97 us
    pallas_call x1, Pallas kernels, local(): pl.pallas_call(interp_kernel, out_shape=jax.ShapeDtypeStruct((total_field...  4.67 us
    unnamed x14, local copies, waits for them, and re-layouts  4.15 us
    pallas_call x1, Pallas kernels, local(): pl.pallas_call(table_kernel, out_shape=jax.ShapeDtypeStruct((waves * part...  3.44 us
  transfers between devices with their start and end apart: 1, of which 1 were waited for; matrix products, arithmetic and copies ran while one was open for 0% of the time, Pallas kernels for 5%

profile of v3, /device:TPU:1, one launch (start us, length us, event | category | flops | bytes accessed | tf_op | source)
XLA Modules:
  0.0 70.3 jit_solution(2453438088049368164)
XLA Ops:
  0.0 0.0 copy-start.6
  0.0 5.0 %legendre.1 = bf16[48,16,128]{2,1,0:T(8,128)(2,1)} custom-call(s32[256]{0:T(256)} %wave_hbm.1, bf16[16,2,4,1280]{3,2,1,0:T(4,128)(2,1)} %spec_hbm.1, bf16[16,128,1280]{2,1,0:T(8,128)(2,1)} %leg_hbm.1), custom_call_target="tpu_custom_call" | custom-call | flops 671088640 | bytes 6291456 | tf_op jit(solution)/shard_map/legendre/pallas_call | solution.py:249
  5.0 21.1 %all-to-all-start = ((bf16[48,16,128]{2,1,0:T(8,128)(2,1)}), bf16[48,16,128]{2,1,0:T(8,128)(2,1)S(1)}, u32[]{:S(2)}, u32[]{:S(2)}) async-start(bf16[48,16,128]{2,1,0:T(8,128)(2,1)} %legendre.1), calls=%async_computation | async-start | bytes 393216 | tf_op jit(solution)/shard_map/all_to_all | solution.py:268
  26.1 0.0 copy-done.6
  26.2 0.1 broadcast_in_dim.6
  26.3 0.1 convert_element_type.18.wave_ref
  26.4 0.0 copy-start.2
  26.4 0.0 copy-start.3
  26.4 0.0 copy-start.4
  26.4 0.0 copy-start.5
  26.4 3.4 %table.1.table_ref = bf16[512,4096]{1,0:T(8,128)(2,1)S(1)} custom-call(f32[512,1]{1,0:T(8,128)S(1)} %convert_element_type.18.wave_ref, f32[1,128]{1,0:T(1,128)S(1)} %fusion.3.start_ref), custom_call_target="tpu_custom_call" | custom-call | flops 20971520 | bytes 4194304 | tf_op jit(solution)/shard_map/table/pallas_call | solution.py:282
  29.9 0.0 copy-start
  29.9 1.9 %copy-done = bf16[512,4096]{1,0:T(8,128)(2,1)} copy-done((bf16[512,4096]{1,0:T(8,128)(2,1)}, bf16[512,4096]{1,0:T(8,128)(2,1)S(1)}, u32[]{:S(2)}) %copy-start) | copy-done | bytes 4194328
  31.8 8.2 %all-to-all-done.four_ref = bf16[48,16,128]{2,1,0:T(8,128)(2,1)S(1)} async-done(((bf16[48,16,128]{2,1,0:T(8,128)(2,1)}), bf16[48,16,128]{2,1,0:T(8,128)(2,1)S(1)}, u32[]{:S(2)}, u32[]{:S(2)}) %all-to-all-start) | async-done | bytes 196640 | tf_op jit(solution)/shard_map/all_to_all | solution.py:268
  40.1 0.0 copy-start.1
  40.1 2.2 %copy-done.1 = bf16[512,4096]{1,0:T(8,128)(2,1)S(1)} copy-done((bf16[512,4096]{1,0:T(8,128)(2,1)S(1)}, bf16[512,4096]{1,0:T(8,128)(2,1)}, u32[]{:S(2)}) %copy-start.1) | copy-done | bytes 4194328
  42.3 0.9 %fourier.1 = bf16[16,120,128]{2,1,0:T(8,128)(2,1)S(1)} custom-call(bf16[48,16,128]{2,1,0:T(8,128)(2,1)S(1)} %all-to-all-done.four_ref, bf16[512,4096]{1,0:T(8,128)(2,1)S(1)} %copy-done.1), custom_call_target="tpu_custom_call" | custom-call | flops 301989888 | bytes 3145728 | tf_op jit(solution)/shard_map/fourier/pallas_call | solution.py:296
  43.2 22.4 %all_to_all.10.grid_ref = bf16[16,120,128]{2,1,0:T(8,128)(2,1)S(1)} all-to-all(bf16[16,120,128]{2,1,0:T(8,128)(2,1)S(1)} %fourier.1), channel_id=1, replica_groups={{0,12,24,36,1,13,25,37,2,14,26,38,3,15,27,39},{4,16,28,40,5,17,29,41,6,..., dimensions={0} | all-to-all | bytes 983040 | tf_op jit(solution)/shard_map/all_to_all | solution.py:310
  65.6 0.0 copy-done.2
  65.6 0.0 copy-done.3
  65.6 0.0 copy-done.4
  65.6 0.0 copy-done.5
  65.6 4.7 %interp.1 = f32[192,8,96]{2,1,0:T(8,128)} custom-call(bf16[16,120,128]{2,1,0:T(8,128)(2,1)S(1)} %all_to_all.10.grid_ref, s32[8,96]{1,0:T(8,128)S(1)} %copy-done.2, s32[8,96]{1,0:T(8,128)S(1)} %copy-done.3, f32[8,96]{1,0:T(8,128)S(1)} %copy-done.4, f32[8,96]{1,0:T(8,128)S(1)} %copy-done.5), custom_call_target="tpu_custom_call" | custom-call | flops 9830400 | bytes 2097152 | tf_op jit(solution)/shard_map/interp/pallas_call | solution.py:314
  (2 shorter events, 0.0 us)
Async XLA Ops:
  0.0 26.1 %copy-start.6 = (s32[256]{0:T(256)S(1)}, s32[256]{0:T(256)}, u32[]{:S(2)}) copy-start(s32[256]{0:T(256)} %wave_hbm.1) | copy-start | bytes 3076
  5.0 35.1 %all-to-all-start = ((bf16[48,16,128]{2,1,0:T(8,128)(2,1)}), bf16[48,16,128]{2,1,0:T(8,128)(2,1)S(1)}, u32[]{:S(2)}, u32[]{:S(2)}) async-start(bf16[48,16,128]{2,1,0:T(8,128)(2,1)} %legendre.1), calls=%async_computation | async-start | bytes 393216 | tf_op jit(solution)/shard_map/all_to_all | solution.py:268
  26.4 39.2 %copy-start.2 = (s32[8,96]{1,0:T(8,128)S(1)}, s32[8,96]{1,0:T(8,128)}, u32[]{:S(2)}) copy-start(s32[8,96]{1,0:T(8,128)} %dep_row.1) | copy-start | bytes 9220
  26.4 39.2 %copy-start.3 = (s32[8,96]{1,0:T(8,128)S(1)}, s32[8,96]{1,0:T(8,128)}, u32[]{:S(2)}) copy-start(s32[8,96]{1,0:T(8,128)} %dep_col.1) | copy-start | bytes 9220
  26.4 39.2 %copy-start.4 = (f32[8,96]{1,0:T(8,128)S(1)}, f32[8,96]{1,0:T(8,128)}, u32[]{:S(2)}) copy-start(f32[8,96]{1,0:T(8,128)} %frac_row.1) | copy-start | bytes 9220
  26.4 39.2 %copy-start.5 = (f32[8,96]{1,0:T(8,128)S(1)}, f32[8,96]{1,0:T(8,128)}, u32[]{:S(2)}) copy-start(f32[8,96]{1,0:T(8,128)} %frac_col.1) | copy-start | bytes 9220
  29.9 1.9 %copy-start = (bf16[512,4096]{1,0:T(8,128)(2,1)}, bf16[512,4096]{1,0:T(8,128)(2,1)S(1)}, u32[]{:S(2)}) copy-start(bf16[512,4096]{1,0:T(8,128)(2,1)S(1)} %table.1.table_ref) | copy-start | bytes 12582916
  40.1 2.2 %copy-start.1 = (bf16[512,4096]{1,0:T(8,128)(2,1)S(1)}, bf16[512,4096]{1,0:T(8,128)(2,1)}, u32[]{:S(2)}) copy-start(bf16[512,4096]{1,0:T(8,128)(2,1)} %copy-done) | copy-start | bytes 12582916

commit v4 on v3

--- a/solution.py
+++ b/solution.py
@@ -15,6 +15,7 @@
 TAPS = 2 * HW + 1
 WIN = 12
 SLAB = 16
+QUAD = 4
 CHUNKS = 1
 WIDE = 64
 SPLIT = WIDE - 2 * HW
@@ -74,7 +75,14 @@
     pad_ref[HW : HW + lats, :] = four
     bands = out_ref.shape[0] // J
     for b in range(bands):
-        tile = pad_ref[b * (lats // bands) : b * (lats // bands) + SLAB, :].astype(jnp.bfloat16)
+        first_row = b * (lats // bands)
+        tile = jnp.concatenate(
+            [
+                pad_ref[first_row + g * QUAD : first_row + (g + 1) * QUAD, :]
+                for g in range(WIN // QUAD)
+            ],
+            axis=1,
+        ).astype(jnp.bfloat16)
         for j in range(J):
             out_ref[b * J + j] = tile
 
@@ -97,23 +105,19 @@
     return cos_value, sin_value
 
 
-def table_kernel(wave_ref, start_ref, out_ref):
+def fill_table(wave_ref, start_ref, out_ref):
     rows = out_ref.shape[0]
     wave = wave_ref[...]
     lane = lax.broadcasted_iota(jnp.int32, (rows, LANES), 1)
     part = (lax.broadcasted_iota(jnp.int32, (rows, LANES), 0) % 2).astype(jnp.float32)
     weight = jnp.where(wave == 0.0, 1.0, 2.0)
-    column_a = lane & (WIDE - 1)
-    column_b = jnp.where(lane < THIN, lane, jnp.where(lane < 2 * THIN, lane - THIN, lane - 2 * THIN))
-    column_b = column_b + SPLIT
-    inner = [turn_parts(wave * column.astype(jnp.float32)) for column in (column_a, column_b)]
+    cos_in, sin_in = turn_parts(wave * lane.astype(jnp.float32))
     cos_out, sin_out = turn_parts(wave * start_ref[...] + part * (NLON // 4))
     cos_out, sin_out = weight * cos_out, weight * sin_out
     for p in range(PEERS):
-        cos_p, sin_p = cos_out[:, p : p + 1], sin_out[:, p : p + 1]
-        for n, (cos_in, sin_in) in enumerate(inner):
-            first = (2 * p + n) * LANES
-            out_ref[:, first : first + LANES] = (cos_p * cos_in - sin_p * sin_in).astype(jnp.bfloat16)
+        out_ref[:, p * LANES : (p + 1) * LANES] = (
+            cos_out[:, p : p + 1] * cos_in - sin_out[:, p : p + 1] * sin_in
+        ).astype(jnp.bfloat16)
 
 
 def fourier_kernel(four_ref, table_ref, out_ref, flat_ref):
@@ -127,43 +131,45 @@
                 four_ref[(per_tile * q + i) * J + j].astype(jnp.float32) for i in range(per_tile)
             ]
             for f in range(fields):
-                piece = jnp.concatenate(
-                    [block[:WIN, f * width : (f + 1) * width] for block in blocks], axis=1
-                )
                 row = (j * fields + f) * WIN
-                flat_ref[row : row + WIN, q * LANES : (q + 1) * LANES] = piece
+                for g in range(WIN // QUAD):
+                    lanes = slice(g * LANES + f * width, g * LANES + (f + 1) * width)
+                    piece = jnp.concatenate([block[:, lanes] for block in blocks], axis=1)
+                    first = row + g * QUAD
+                    flat_ref[first : first + QUAD, q * LANES : (q + 1) * LANES] = piece
     flat = flat_ref[...].astype(jnp.bfloat16)
     depth = flat.shape[0]
     half, third = depth // 2, depth // 3
     in_low = lax.broadcasted_iota(jnp.int32, (half, LANES), 1) < WIDE
     lane = lax.broadcasted_iota(jnp.int32, (third, LANES), 1)
-    for p in range(PEERS):
+    for n in range(PEERS // 2):
         both = jnp.dot(
             flat,
-            table_ref[:, 2 * p * LANES : 2 * (p + 1) * LANES],
+            table_ref[:, 2 * n * LANES : 2 * (n + 1) * LANES],
             preferred_element_type=jnp.float32,
         )
-        wide, thin = both[:, :LANES], both[:, LANES:]
-        wide = jnp.where(in_low, wide[:half], wide[half:])
-        thin = jnp.where(
-            lane < THIN,
-            thin[:third],
-            jnp.where(lane < 2 * THIN, thin[third : 2 * third], thin[2 * third :]),
-        )
-        out_ref[p] = jnp.concatenate([wide, thin], axis=0).astype(jnp.bfloat16)
-
-
-def interp_kernel(grid_ref, dep_row, dep_col, frac_row, frac_col, out_ref, buf, weight_ref):
+        for m in range(2):
+            rows = both[:, m * LANES : (m + 1) * LANES]
+            wide = jnp.where(in_low, rows[:half], pltpu.roll(rows[half:], WIDE, 1))
+            thins = [
+                pltpu.roll(rows[k * third : (k + 1) * third], (k * THIN - SPLIT) % LANES, 1)
+                for k in range(3)
+            ]
+            thin = jnp.where(lane < THIN, thins[0], jnp.where(lane < 2 * THIN, thins[1], thins[2]))
+            out_ref[2 * n + m] = jnp.concatenate([wide, thin], axis=0).astype(jnp.bfloat16)
+
+
+def tables_kernel(
+    wave_ref, start_ref, dep_row, dep_col, frac_row, frac_col, table_ref, out_ref, pad_ref
+):
+    fill_table(wave_ref, start_ref, table_ref)
     rows, cols = dep_row.shape
-    fields = 4
     row_ids = lax.axis_index("band") * rows + lax.broadcasted_iota(jnp.int32, (rows, cols), 0)
     col_ids = lax.axis_index("field") * cols + lax.broadcasted_iota(jnp.int32, (rows, cols), 1)
     delta_row = dep_row[...] - row_ids
     delta_col = dep_col[...] - col_ids + HW
     delta_col = jnp.where(delta_col < 0, delta_col + NLON, delta_col)
     delta_col = jnp.where(delta_col >= NLON, delta_col - NLON, delta_col) - HW
-    a = frac_row[...]
-    b = frac_col[...]
 
     def hats(delta, frac):
         return [
@@ -171,41 +177,52 @@
             for o in range(-HW, HW + 1)
         ]
 
-    row_hats, col_hats = hats(delta_row, a), hats(delta_col, b)
-    scratch = weight_ref.shape[0] - 1
-    weight_ref[scratch] = jnp.zeros((rows, LANES), jnp.float32)
+    row_hats, col_hats = hats(delta_row, frac_row[...]), hats(delta_col, frac_col[...])
+    pad_ref[...] = jnp.zeros_like(pad_ref)
     lane = lax.broadcasted_iota(jnp.int32, (rows, LANES), 1)
     for d in range(TAPS):
         for e in range(TAPS):
-            weight_ref[scratch, :, :cols] = row_hats[d] * col_hats[e]
-            tap = weight_ref[scratch]
+            pad_ref[:, :cols] = row_hats[d] * col_hats[e]
+            tap = pad_ref[...]
             wide = jnp.where(lane < SPLIT, tap, 0.0)
             thin = pltpu.roll(jnp.where(lane < SPLIT, 0.0, tap), LANES - SPLIT, 1)
             wide = wide + pltpu.roll(wide, WIDE, 1)
             thin = thin + pltpu.roll(thin, THIN, 1) + pltpu.roll(thin, 2 * THIN, 1)
-            weight_ref[d * TAPS + e] = pltpu.roll(wide, e, 1) if e else wide
-            weight_ref[TAPS * TAPS + d * TAPS + e] = pltpu.roll(thin, e, 1) if e else thin
-    depth = grid_ref.shape[1]
-    per_peer = J * fields
-    for p in range(PEERS):
+            out_ref[d * TAPS + e] = pltpu.roll(wide, e, 1) if e else wide
+            out_ref[TAPS * TAPS + d * TAPS + e] = pltpu.roll(thin, e, 1) if e else thin
+
+
+def interp_kernel(grid_ref, taps_ref, out_ref, buf):
+    rows, cols = out_ref.shape[1:]
+    peers, depth = grid_ref.shape[:2]
+    per_peer = out_ref.shape[0] // peers
+    fields = per_peer // J
+    lane = lax.broadcasted_iota(jnp.int32, (rows, LANES), 1)
+    for p in range(peers):
         buf[p * depth : (p + 1) * depth, :] = grid_ref[p].astype(jnp.float32)
 
-    def stencil(base, first_tap):
-        planes = [buf[pl.ds(base + d, rows), :] for d in range(TAPS)]
-        result = None
-        for e in range(TAPS):
-            column = planes[0] * weight_ref[first_tap + e]
-            for d in range(1, TAPS):
-                column = column + planes[d] * weight_ref[first_tap + d * TAPS + e]
-            column = pltpu.roll(column, LANES - e, 1) if e else column
-            result = column if result is None else result + column
-        return result
+    def stencils(bases, first_tap):
+        sums = [[None] * TAPS for _ in bases]
+        for d in range(TAPS):
+            planes = [buf[pl.ds(base + d, rows), :] for base in bases]
+            for e in range(TAPS):
+                tap = taps_ref[first_tap + d * TAPS + e]
+                for n, plane in enumerate(planes):
+                    term = plane * tap
+                    sums[n][e] = term if d == 0 else sums[n][e] + term
+        results = []
+        for columns in sums:
+            result = columns[0]
+            for e in range(1, TAPS):
+                result = result + pltpu.roll(columns[e], LANES - e, 1)
+            results.append(result)
+        return results
 
     def body(p, carry):
         base = pl.multiple_of(p * depth, 8)
-        wide = [stencil(base + u * WIN, 0) for u in range(per_peer // 2)]
+        wide = stencils([base + u * WIN for u in range(per_peer // 2)], 0)
         low = base + (per_peer // 2) * WIN
-        thin = [stencil(low + v * WIN, TAPS * TAPS) for v in range(per_peer // 3)]
+        thin = stencils([low + v * WIN for v in range(per_peer // 3)], TAPS * TAPS)
         for t in range(per_peer):
             left = wide[t % (per_peer // 2)]
             left = pltpu.roll(left, WIDE, 1) if t >= per_peer // 2 else left
@@ -216,7 +233,7 @@
             out_ref[row] = jnp.where(lane < SPLIT, left, right)[:, :cols]
         return carry
 
-    lax.fori_loop(0, PEERS, body, 0)
+    lax.fori_loop(0, peers, body, 0, unroll=4)
 
 
 def exchange_groups(bands):
@@ -248,7 +265,7 @@
 
     four = pl.pallas_call(
         legendre_kernel,
-        out_shape=jax.ShapeDtypeStruct((bands * J, SLAB, LANES), jnp.bfloat16),
+        out_shape=jax.ShapeDtypeStruct((bands * J, QUAD, WIN // QUAD * LANES), jnp.bfloat16),
         in_specs=[hbm, hbm, hbm],
         out_specs=vmem,
         scratch_shapes=[
@@ -279,17 +296,28 @@
     start = ((peer % XS) * ZS + z_peer) * cols - HW
     start = jnp.where(start < 0, start + NLON, start)
     wave_rows = jnp.broadcast_to(wavenum[:, None], (waves, parts)).reshape(waves * parts, 1)
-    table = pl.pallas_call(
-        table_kernel,
-        out_shape=jax.ShapeDtypeStruct((waves * parts, 2 * PEERS * LANES), jnp.bfloat16),
-        in_specs=[vmem, vmem],
-        out_specs=vmem,
+    table, taps = pl.pallas_call(
+        tables_kernel,
+        out_shape=[
+            jax.ShapeDtypeStruct((waves * parts, PEERS * LANES), jnp.bfloat16),
+            jax.ShapeDtypeStruct((2 * TAPS * TAPS, rows, LANES), jnp.float32),
+        ],
+        in_specs=[vmem] * 6,
+        out_specs=[vmem] * 2,
+        scratch_shapes=[pltpu.VMEM((rows, LANES), jnp.float32)],
         compiler_params=pltpu.CompilerParams(vmem_limit_bytes=24 * MIB),
         cost_estimate=pl.CostEstimate(
-            flops=20 * MIB, bytes_accessed=4 * MIB, transcendentals=MIB // 4
-        ),
-        name="table",
-    )(wave_rows.astype(jnp.float32), start.astype(jnp.float32)[None, :])
+            flops=20 * MIB, bytes_accessed=4 * MIB, transcendentals=0
+        ),
+        name="tables",
+    )(
+        wave_rows.astype(jnp.float32),
+        start.astype(jnp.float32)[None, :],
+        dep_row,
+        dep_col,
+        frac_row,
+        frac_col,
+    )
 
     depth = J * fields * WIN
     packed = depth // 2 + depth // 3
@@ -314,18 +342,15 @@
     return pl.pallas_call(
         interp_kernel,
         out_shape=jax.ShapeDtypeStruct((total_fields, rows, cols), jnp.float32),
-        in_specs=[vmem] * 5,
+        in_specs=[vmem] * 2,
         out_specs=vmem,
-        scratch_shapes=[
-            pltpu.VMEM((PEERS * packed, LANES), jnp.float32),
-            pltpu.VMEM((2 * TAPS * TAPS + 1, rows, LANES), jnp.float32),
-        ],
+        scratch_shapes=[pltpu.VMEM((PEERS * packed, LANES), jnp.float32)],
         compiler_params=pltpu.CompilerParams(vmem_limit_bytes=24 * MIB),
         cost_estimate=pl.CostEstimate(
             flops=50 * total_fields * rows * LANES, bytes_accessed=2 * MIB, transcendentals=0
         ),
         name="interp",
-    )(segment, dep_row, dep_col, frac_row, frac_col)
+    )(segment, taps)
 
 
 def solution(mesh):

time: 70.5 us -> 65 us (0.922)
  local copies, waits for them, and re-layouts: 4.34 us -> 0.21 us
  Pallas kernels: 14 us -> 13 us
    unnamed x14 -> x10, local copies, waits for them, and re-layouts: 4.15 us -> 0.02 us
    pallas_call x1, Pallas kernels: 4.67 us -> 3.14 us  [local(): pl.pallas_call(interp_kernel, out_shape=jax.ShapeDtypeStruct((total_field...]
  transfers between devices with their start and end apart: 1 -> 1, of which waited for: 1 -> 1; matrix products, arithmetic and copies ran while one was open for 0% -> 0% of each run, Pallas kernels for 5% -> 6%
where the time goes in v4:
time: 65 us; the launch traced here: 64.8 us
  blocking collectives  22.2 us (34%)
  starting transfers between devices  21.1 us (32%)
  Pallas kernels  13 us (20%)
  waiting for transfers between devices  8.1 us (12%)
    all_to_all x1, blocking collectives, local(): lax.all_to_all(grid, ('band', 'field'), split_axis=0, concat_axis=0, tile...  22.2 us
    all_to_all x1, starting transfers between devices, local(): lax.all_to_all(four, ('band', 'field'), split_axis=0, concat_axis=0, tile...  21.1 us
    all_to_all x1, waiting for transfers between devices, local(): lax.all_to_all(four, ('band', 'field'), split_axis=0, concat_axis=0, tile...  8.1 us
    pallas_call x1, Pallas kernels, local(): pl.pallas_call(legendre_kernel, out_shape=jax.ShapeDtypeStruct((bands * J...  4.98 us
    pallas_call x1, Pallas kernels, local(): pl.pallas_call(tables_kernel, out_shape=[jax.ShapeDtypeStruct((waves * pa...  4.07 us
    pallas_call x1, Pallas kernels, local(): pl.pallas_call(interp_kernel, out_shape=jax.ShapeDtypeStruct((total_field...  3.14 us
  transfers between devices with their start and end apart: 1, of which 1 were waited for; matrix products, arithmetic and copies ran while one was open for 0% of the time, Pallas kernels for 6%

profile of v4, /device:TPU:1, one launch (start us, length us, event | category | flops | bytes accessed | tf_op | source)
XLA Modules:
  0.0 64.8 jit_solution(643298607872742687)
XLA Ops:
  0.0 0.0 copy-start.4
  0.0 0.0 copy-start.3
  0.0 0.0 copy-start.2
  0.0 0.0 copy-start.1
  0.0 0.0 copy-start
  0.0 5.0 %legendre.1 = bf16[48,4,384]{2,1,0:T(4,128)(2,1)} custom-call(s32[256]{0:T(256)} %wave_hbm.1, bf16[16,2,4,1280]{3,2,1,0:T(4,128)(2,1)} %spec_hbm.1, bf16[16,128,1280]{2,1,0:T(8,128)(2,1)} %leg_hbm.1), custom_call_target="tpu_custom_call" | custom-call | flops 671088640 | bytes 6291456 | tf_op jit(solution)/shard_map/legendre/pallas_call | solution.py:266
  5.0 21.1 %all-to-all-start = ((bf16[48,4,384]{2,1,0:T(4,128)(2,1)}), bf16[48,4,384]{2,1,0:T(4,128)(2,1)S(1)}, u32[]{:S(2)}, u32[]{:S(2)}) async-start(bf16[48,4,384]{2,1,0:T(4,128)(2,1)} %legendre.1), calls=%async_computation | async-start | bytes 294912 | tf_op jit(solution)/shard_map/all_to_all | solution.py:285
  26.2 0.0 copy-done.4
  26.2 0.1 broadcast_in_dim.6
  26.3 0.1 convert_element_type.18.wave_ref
  26.4 0.0 copy-done.3
  26.4 0.0 copy-done.2
  26.5 0.0 copy-done.1
  26.5 0.0 copy-done
  26.5 4.1 %tables.1 = (bf16[512,2048]{1,0:T(8,128)(2,1)S(1)}, f32[50,8,128]{2,1,0:T(8,128)S(1)}) custom-call(f32[512,1]{1,0:T(8,128)S(1)} %convert_element_type.18.wave_ref, f32[1,128]{1,0:T(1,128)S(1)} %fusion.3.start_ref, s32[8,96]{1,0:T(8,128)S(1)} %copy-done, s32[8,96]{1,0:T(8,128)S(1)} %copy-done.1, f32[8,96]{1,0:T(8,128)S(1)} %copy-done.2, f32[8,96]{1,0:T(8,128)S(1)} %copy-done.3), custom_call_target="tpu_custom_call" | custom-call | flops 20971520 | bytes 4194304 | tf_op jit(solution)/shard_map/tables/pallas_call | solution.py:299
  30.6 8.1 %all-to-all-done.four_ref = bf16[48,4,384]{2,1,0:T(4,128)(2,1)S(1)} async-done(((bf16[48,4,384]{2,1,0:T(4,128)(2,1)}), bf16[48,4,384]{2,1,0:T(4,128)(2,1)S(1)}, u32[]{:S(2)}, u32[]{:S(2)}) %all-to-all-start) | async-done | bytes 147488 | tf_op jit(solution)/shard_map/all_to_all | solution.py:285
  38.7 0.8 %fourier.1 = bf16[16,120,128]{2,1,0:T(8,128)(2,1)S(1)} custom-call(bf16[48,4,384]{2,1,0:T(4,128)(2,1)S(1)} %all-to-all-done.four_ref, bf16[512,2048]{1,0:T(8,128)(2,1)S(1)} %get-tuple-element.7.table_ref), custom_call_target="tpu_custom_call" | custom-call | flops 301989888 | bytes 3145728 | tf_op jit(solution)/shard_map/fourier/pallas_call | solution.py:324
  39.5 22.2 %all_to_all.10.grid_ref = bf16[16,120,128]{2,1,0:T(8,128)(2,1)S(1)} all-to-all(bf16[16,120,128]{2,1,0:T(8,128)(2,1)S(1)} %fourier.1), channel_id=1, replica_groups={{0,12,24,36,1,13,25,37,2,14,26,38,3,15,27,39},{4,16,28,40,5,17,29,41,6,..., dimensions={0} | all-to-all | bytes 983040 | tf_op jit(solution)/shard_map/all_to_all | solution.py:338
  61.7 3.1 %interp.1 = f32[192,8,96]{2,1,0:T(8,128)} custom-call(bf16[16,120,128]{2,1,0:T(8,128)(2,1)S(1)} %all_to_all.10.grid_ref, f32[50,8,128]{2,1,0:T(8,128)S(1)} %get-tuple-element.8.taps_ref), custom_call_target="tpu_custom_call" | custom-call | flops 9830400 | bytes 2097152 | tf_op jit(solution)/shard_map/interp/pallas_call | solution.py:342
  (2 shorter events, 0.0 us)
Async XLA Ops:
  0.0 26.2 %copy-start.4 = (s32[256]{0:T(256)S(1)}, s32[256]{0:T(256)}, u32[]{:S(2)}) copy-start(s32[256]{0:T(256)} %wave_hbm.1) | copy-start | bytes 3076
  0.0 26.4 %copy-start.3 = (f32[8,96]{1,0:T(8,128)S(1)}, f32[8,96]{1,0:T(8,128)}, u32[]{:S(2)}) copy-start(f32[8,96]{1,0:T(8,128)} %frac_col.1) | copy-start | bytes 9220
  0.0 26.4 %copy-start.2 = (f32[8,96]{1,0:T(8,128)S(1)}, f32[8,96]{1,0:T(8,128)}, u32[]{:S(2)}) copy-start(f32[8,96]{1,0:T(8,128)} %frac_row.1) | copy-start | bytes 9220
  0.0 26.5 %copy-start.1 = (s32[8,96]{1,0:T(8,128)S(1)}, s32[8,96]{1,0:T(8,128)}, u32[]{:S(2)}) copy-start(s32[8,96]{1,0:T(8,128)} %dep_col.1) | copy-start | bytes 9220
  0.0 26.5 %copy-start = (s32[8,96]{1,0:T(8,128)S(1)}, s32[8,96]{1,0:T(8,128)}, u32[]{:S(2)}) copy-start(s32[8,96]{1,0:T(8,128)} %dep_row.1) | copy-start | bytes 9220
  5.0 33.6 %all-to-all-start = ((bf16[48,4,384]{2,1,0:T(4,128)(2,1)}), bf16[48,4,384]{2,1,0:T(4,128)(2,1)S(1)}, u32[]{:S(2)}, u32[]{:S(2)}) async-start(bf16[48,4,384]{2,1,0:T(4,128)(2,1)} %legendre.1), calls=%async_computation | async-start | bytes 294912 | tf_op jit(solution)/shard_map/all_to_all | solution.py:285

commit v5 on v4

--- a/solution.py
+++ b/solution.py
@@ -16,7 +16,7 @@
 WIN = 12
 SLAB = 16
 QUAD = 4
-CHUNKS = 1
+CHUNK = 768
 WIDE = 64
 SPLIT = WIDE - 2 * HW
 THIN = 40
@@ -25,25 +25,34 @@
 
 
 def legendre_kernel(
-    wave_hbm, spec_hbm, leg_hbm, out_ref, wave_ref, spec_buf, leg_buf, pad_ref, small_sem, leg_sem
+    wave_hbm,
+    spec_hbm,
+    leg_hbm,
+    out_ref,
+    wave_ref,
+    spec_buf,
+    leg_buf,
+    weight_ref,
+    sum_ref,
+    pad_ref,
+    small_sem,
+    leg_sem,
 ):
     slots, parts, fields, degrees = spec_buf.shape
     lats = leg_buf.shape[1]
     group = parts * fields
-    chunks = leg_sem.shape[0]
-    per_chunk = slots // chunks
     wave_copy = pltpu.make_async_copy(wave_hbm, wave_ref, small_sem.at[0])
     spec_copy = pltpu.make_async_copy(spec_hbm, spec_buf, small_sem.at[1])
+    wave_copy.start()
     spec_copy.start()
-    wave_copy.start()
-    leg_copies = []
-    for c in range(chunks):
-        part = pl.ds(c * per_chunk, per_chunk)
-        leg_copies.append(
-            pltpu.make_async_copy(leg_hbm.at[part], leg_buf.at[part], leg_sem.at[c])
-        )
-    for copy in leg_copies:
-        copy.start()
+    low_copy = pltpu.make_async_copy(
+        leg_hbm.at[:, :, pl.ds(0, CHUNK)], leg_buf.at[:, :, pl.ds(0, CHUNK)], leg_sem.at[0]
+    )
+    rest = degrees - CHUNK
+    high_copy = pltpu.make_async_copy(
+        leg_hbm.at[:, :, pl.ds(CHUNK, rest)], leg_buf.at[:, :, pl.ds(CHUNK, rest)], leg_sem.at[1]
+    )
+    low_copy.start()
     first = lax.axis_index("band") * slots
     pad_ref[:8, :] = jnp.zeros((8, LANES), jnp.float32)
     pad_ref[lats:, :] = jnp.zeros((SLAB, LANES), jnp.float32)
@@ -54,23 +63,44 @@
     position = lax.broadcasted_iota(jnp.int32, (group, degrees), 1)
     slot_of_lane = lax.broadcasted_iota(jnp.int32, (lats, LANES), 1) // group
     wave_copy.wait()
+    needs_high = degrees - wave_ref[first] > CHUNK
+
+    @pl.when(needs_high)
+    def _():
+        high_copy.start()
+
     spec_copy.wait()
     kept = []
     for s in range(slots):
         part = spec_buf[s].astype(jnp.float32)
         rows = jnp.concatenate([part[0], part[1]], axis=0)
         kept.append(jnp.where(position < degrees - wave_ref[first + s], rows, 0.0))
-    weights = jnp.concatenate(kept, axis=0).astype(jnp.bfloat16)
-    total = jnp.zeros((lats, LANES), jnp.float32)
-    for c in range(chunks):
-        leg_copies[c].wait()
-        rows = leg_buf[c * per_chunk : (c + 1) * per_chunk].reshape(per_chunk * lats, degrees)
-        products = lax.dot_general(
-            rows, weights, (((1,), (1,)), ((), ())), preferred_element_type=jnp.float32
+    weight_ref[...] = jnp.concatenate(kept, axis=0).astype(jnp.bfloat16)
+
+    def products_of(start, width):
+        return lax.dot_general(
+            leg_buf[:, :, start : start + width].reshape(slots * lats, width),
+            weight_ref[:, start : start + width],
+            (((1,), (1,)), ((), ())),
+            preferred_element_type=jnp.float32,
         )
-        for n in range(per_chunk):
-            own = slot_of_lane == c * per_chunk + n
-            total = jnp.where(own, products[n * lats : (n + 1) * lats], total)
+
+    def own_lanes(products):
+        kept_lanes = jnp.zeros((lats, LANES), jnp.float32)
+        for s in range(slots):
+            part = products[s * lats : (s + 1) * lats]
+            kept_lanes = jnp.where(slot_of_lane == s, part, kept_lanes)
+        return kept_lanes
+
+    low_copy.wait()
+    sum_ref[...] = own_lanes(products_of(0, CHUNK))
+
+    @pl.when(needs_high)
+    def _():
+        high_copy.wait()
+        sum_ref[...] += own_lanes(products_of(CHUNK, rest))
+
+    total = sum_ref[...]
     four = jnp.dot(total.astype(jnp.bfloat16), perm, preferred_element_type=jnp.float32)
     pad_ref[HW : HW + lats, :] = four
     bands = out_ref.shape[0] // J
@@ -84,7 +114,7 @@
             axis=1,
         ).astype(jnp.bfloat16)
         for j in range(J):
-            out_ref[b * J + j] = tile
+            out_ref[j * bands + b] = tile
 
 
 def turn_parts(product):
@@ -128,7 +158,7 @@
     for j in range(J):
         for q in range(bands // per_tile):
             blocks = [
-                four_ref[(per_tile * q + i) * J + j].astype(jnp.float32) for i in range(per_tile)
+                four_ref[j * bands + per_tile * q + i].astype(jnp.float32) for i in range(per_tile)
             ]
             for f in range(fields):
                 row = (j * fields + f) * WIN
@@ -192,7 +222,7 @@
             out_ref[TAPS * TAPS + d * TAPS + e] = pltpu.roll(thin, e, 1) if e else thin
 
 
-def interp_kernel(grid_ref, taps_ref, out_ref, buf):
+def interp_kernel(grid_ref, taps_ref, out_hbm, buf, out_ref, out_sem):
     rows, cols = out_ref.shape[1:]
     peers, depth = grid_ref.shape[:2]
     per_peer = out_ref.shape[0] // peers
@@ -218,7 +248,7 @@
             results.append(result)
         return results
 
-    def body(p, carry):
+    def one_peer(p, x, i):
         base = pl.multiple_of(p * depth, 8)
         wide = stencils([base + u * WIN for u in range(per_peer // 2)], 0)
         low = base + (per_peer // 2) * WIN
@@ -228,12 +258,22 @@
             left = pltpu.roll(left, WIDE, 1) if t >= per_peer // 2 else left
             right = thin[t % (per_peer // 3)]
             right = pltpu.roll(right, (SPLIT - THIN * (t // (per_peer // 3))) % LANES, 1)
-            z = p // XS + ZC * (t // fields)
-            row = ((p % XS) * ZS + z) * fields + t % fields
+            row = (x * ZS + i + ZC * (t // fields)) * fields + t % fields
             out_ref[row] = jnp.where(lane < SPLIT, left, right)[:, :cols]
+
+    def part_copy(x):
+        part = pl.ds(x * (ZS * fields), ZS * fields)
+        return pltpu.make_async_copy(out_ref.at[part], out_hbm.at[part], out_sem.at[x])
+
+    def body(x, carry):
+        for i in range(ZC):
+            one_peer(i * XS + x, x, i)
+        part_copy(x).start()
         return carry
 
-    lax.fori_loop(0, peers, body, 0, unroll=4)
+    lax.fori_loop(0, XS, body, 0)
+    for x in range(XS):
+        part_copy(x).wait()
 
 
 def exchange_groups(bands):
@@ -241,7 +281,7 @@
     for x in range(XS):
         for i in range(ZC):
             first.append(
-                [b * XS * ZS + x * ZS + i + ZC * j for b in range(bands) for j in range(J)]
+                [b * XS * ZS + x * ZS + i + ZC * j for j in range(J) for b in range(bands)]
             )
     for b in range(bands):
         shift = ZC // 2 if b % 2 and J > 1 else 0
@@ -272,9 +312,11 @@
             pltpu.SMEM(wavenum.shape, jnp.int32),
             pltpu.VMEM(spectra.shape, jnp.bfloat16),
             pltpu.VMEM(legendre.shape, jnp.bfloat16),
+            pltpu.VMEM((LANES, degrees), jnp.bfloat16),
+            pltpu.VMEM((lats, LANES), jnp.float32),
             pltpu.VMEM((lats + SLAB, LANES), jnp.float32),
             pltpu.SemaphoreType.DMA((2,)),
-            pltpu.SemaphoreType.DMA((CHUNKS,)),
+            pltpu.SemaphoreType.DMA((2,)),
         ],
         compiler_params=pltpu.CompilerParams(vmem_limit_bytes=60 * MIB),
         cost_estimate=pl.CostEstimate(
@@ -343,8 +385,12 @@
         interp_kernel,
         out_shape=jax.ShapeDtypeStruct((total_fields, rows, cols), jnp.float32),
         in_specs=[vmem] * 2,
-        out_specs=vmem,
-        scratch_shapes=[pltpu.VMEM((PEERS * packed, LANES), jnp.float32)],
+        out_specs=hbm,
+        scratch_shapes=[
+            pltpu.VMEM((PEERS * packed, LANES), jnp.float32),
+            pltpu.VMEM((total_fields, rows, cols), jnp.float32),
+            pltpu.SemaphoreType.DMA((XS,)),
+        ],
         compiler_params=pltpu.CompilerParams(vmem_limit_bytes=24 * MIB),
         cost_estimate=pl.CostEstimate(
             flops=50 * total_fields * rows * LANES, bytes_accessed=2 * MIB, transcendentals=0

time: 65 us -> 62.9 us (0.968)
  blocking collectives: 22.2 us -> 20.8 us
  starting transfers between devices: 21.1 us -> 20.4 us
    all_to_all x1, blocking collectives: 22.2 us -> 20.8 us  [local(): lax.all_to_all(grid, ('band', 'field'), split_axis=0, concat_axis=0, tile...]
    all_to_all x1, starting transfers between devices: 21.1 us -> 20.4 us  [local(): lax.all_to_all(four, ('band', 'field'), split_axis=0, concat_axis=0, tile...]
  transfers between devices with their start and end apart: 1 -> 1, of which waited for: 1 -> 1; matrix products, arithmetic and copies ran while one was open for 0% -> 0% of each run, Pallas kernels for 6% -> 7%
where the time goes in v5:
time: 62.9 us; the launch traced here: 62.1 us
  blocking collectives  20.8 us (33%)
  starting transfers between devices  20.4 us (32%)
  Pallas kernels  12.5 us (20%)
  waiting for transfers between devices  7.95 us (13%)
    all_to_all x1, blocking collectives, local(): lax.all_to_all(grid, ('band', 'field'), split_axis=0, concat_axis=0, tile...  20.8 us
    all_to_all x1, starting transfers between devices, local(): lax.all_to_all(four, ('band', 'field'), split_axis=0, concat_axis=0, tile...  20.4 us
    all_to_all x1, waiting for transfers between devices, local(): lax.all_to_all(four, ('band', 'field'), split_axis=0, concat_axis=0, tile...  7.95 us
    pallas_call x1, Pallas kernels, local(): pl.pallas_call(legendre_kernel, out_shape=jax.ShapeDtypeStruct((bands * J...  4.58 us
    pallas_call x1, Pallas kernels, local(): pl.pallas_call(tables_kernel, out_shape=[jax.ShapeDtypeStruct((waves * pa...  4.07 us
    pallas_call x1, Pallas kernels, local(): pl.pallas_call(interp_kernel, out_shape=jax.ShapeDtypeStruct((total_field...  3.02 us
  transfers between devices with their start and end apart: 1, of which 1 were waited for; matrix products, arithmetic and copies ran while one was open for 0% of the time, Pallas kernels for 7%

profile of v5, /device:TPU:1, one launch (start us, length us, event | category | flops | bytes accessed | tf_op | source)
XLA Modules:
  0.0 62.1 jit_solution(319621103681921208)
XLA Ops:
  0.0 0.0 copy-start.4
  0.0 0.0 copy-start.3
  0.0 0.0 copy-start.2
  0.0 0.0 copy-start.1
  0.0 0.0 copy-start
  0.0 4.6 %legendre.1 = bf16[48,4,384]{2,1,0:T(4,128)(2,1)} custom-call(s32[256]{0:T(256)} %wave_hbm.1, bf16[16,2,4,1280]{3,2,1,0:T(4,128)(2,1)} %spec_hbm.1, bf16[16,128,1280]{2,1,0:T(8,128)(2,1)} %leg_hbm.1), custom_call_target="tpu_custom_call" | custom-call | flops 671088640 | bytes 6291456 | tf_op jit(solution)/shard_map/legendre/pallas_call | solution.py:306
  4.6 20.4 %all-to-all-start = ((bf16[48,4,384]{2,1,0:T(4,128)(2,1)}), bf16[48,4,384]{2,1,0:T(4,128)(2,1)S(1)}, u32[]{:S(2)}, u32[]{:S(2)}) async-start(bf16[48,4,384]{2,1,0:T(4,128)(2,1)} %legendre.1), calls=%async_computation | async-start | bytes 294912 | tf_op jit(solution)/shard_map/all_to_all | solution.py:327
  25.1 0.0 copy-done.4
  25.1 0.1 broadcast_in_dim.6
  25.2 0.1 convert_element_type.18.wave_ref
  25.3 0.0 copy-done.3
  25.3 0.0 copy-done.2
  25.4 0.0 copy-done.1
  25.4 0.0 copy-done
  25.4 4.1 %tables.1 = (bf16[512,2048]{1,0:T(8,128)(2,1)S(1)}, f32[50,8,128]{2,1,0:T(8,128)S(1)}) custom-call(f32[512,1]{1,0:T(8,128)S(1)} %convert_element_type.18.wave_ref, f32[1,128]{1,0:T(1,128)S(1)} %fusion.3.start_ref, s32[8,96]{1,0:T(8,128)S(1)} %copy-done, s32[8,96]{1,0:T(8,128)S(1)} %copy-done.1, f32[8,96]{1,0:T(8,128)S(1)} %copy-done.2, f32[8,96]{1,0:T(8,128)S(1)} %copy-done.3), custom_call_target="tpu_custom_call" | custom-call | flops 20971520 | bytes 4194304 | tf_op jit(solution)/shard_map/tables/pallas_call | solution.py:341
  29.5 7.9 %all-to-all-done.four_ref = bf16[48,4,384]{2,1,0:T(4,128)(2,1)S(1)} async-done(((bf16[48,4,384]{2,1,0:T(4,128)(2,1)}), bf16[48,4,384]{2,1,0:T(4,128)(2,1)S(1)}, u32[]{:S(2)}, u32[]{:S(2)}) %all-to-all-start) | async-done | bytes 147488 | tf_op jit(solution)/shard_map/all_to_all | solution.py:327
  37.4 0.8 %fourier.1 = bf16[16,120,128]{2,1,0:T(8,128)(2,1)S(1)} custom-call(bf16[48,4,384]{2,1,0:T(4,128)(2,1)S(1)} %all-to-all-done.four_ref, bf16[512,2048]{1,0:T(8,128)(2,1)S(1)} %get-tuple-element.7.table_ref), custom_call_target="tpu_custom_call" | custom-call | flops 301989888 | bytes 3145728 | tf_op jit(solution)/shard_map/fourier/pallas_call | solution.py:366
  38.2 20.8 %all_to_all.10.grid_ref = bf16[16,120,128]{2,1,0:T(8,128)(2,1)S(1)} all-to-all(bf16[16,120,128]{2,1,0:T(8,128)(2,1)S(1)} %fourier.1), channel_id=1, replica_groups={{0,12,24,36,1,13,25,37,2,14,26,38,3,15,27,39},{4,16,28,40,5,17,29,41,6,..., dimensions={0} | all-to-all | bytes 983040 | tf_op jit(solution)/shard_map/all_to_all | solution.py:380
  59.1 3.0 %interp.1 = f32[192,8,96]{2,1,0:T(8,128)} custom-call(bf16[16,120,128]{2,1,0:T(8,128)(2,1)S(1)} %all_to_all.10.grid_ref, f32[50,8,128]{2,1,0:T(8,128)S(1)} %get-tuple-element.8.taps_ref), custom_call_target="tpu_custom_call" | custom-call | flops 9830400 | bytes 2097152 | tf_op jit(solution)/shard_map/interp/pallas_call | solution.py:384
  (2 shorter events, 0.0 us)
Async XLA Ops:
  0.0 25.1 %copy-start.4 = (s32[256]{0:T(256)S(1)}, s32[256]{0:T(256)}, u32[]{:S(2)}) copy-start(s32[256]{0:T(256)} %wave_hbm.1) | copy-start | bytes 3076
  0.0 25.3 %copy-start.3 = (f32[8,96]{1,0:T(8,128)S(1)}, f32[8,96]{1,0:T(8,128)}, u32[]{:S(2)}) copy-start(f32[8,96]{1,0:T(8,128)} %frac_col.1) | copy-start | bytes 9220
  0.0 25.3 %copy-start.2 = (f32[8,96]{1,0:T(8,128)S(1)}, f32[8,96]{1,0:T(8,128)}, u32[]{:S(2)}) copy-start(f32[8,96]{1,0:T(8,128)} %frac_row.1) | copy-start | bytes 9220
  0.0 25.3 %copy-start.1 = (s32[8,96]{1,0:T(8,128)S(1)}, s32[8,96]{1,0:T(8,128)}, u32[]{:S(2)}) copy-start(s32[8,96]{1,0:T(8,128)} %dep_col.1) | copy-start | bytes 9220
  0.0 25.3 %copy-start = (s32[8,96]{1,0:T(8,128)S(1)}, s32[8,96]{1,0:T(8,128)}, u32[]{:S(2)}) copy-start(s32[8,96]{1,0:T(8,128)} %dep_row.1) | copy-start | bytes 9220
  4.6 32.8 %all-to-all-start = ((bf16[48,4,384]{2,1,0:T(4,128)(2,1)}), bf16[48,4,384]{2,1,0:T(4,128)(2,1)S(1)}, u32[]{:S(2)}, u32[]{:S(2)}) async-start(bf16[48,4,384]{2,1,0:T(4,128)(2,1)} %legendre.1), calls=%async_computation | async-start | bytes 294912 | tf_op jit(solution)/shard_map/all_to_all | solution.py:327

commit v6 on v5

--- a/solution.py
+++ b/solution.py
@@ -242,9 +242,9 @@
                     sums[n][e] = term if d == 0 else sums[n][e] + term
         results = []
         for columns in sums:
-            result = columns[0]
-            for e in range(1, TAPS):
-                result = result + pltpu.roll(columns[e], LANES - e, 1)
+            result = columns[TAPS - 1]
+            for e in range(TAPS - 2, -1, -1):
+                result = columns[e] + pltpu.roll(result, LANES - 1, 1)
             results.append(result)
         return results
 
@@ -271,7 +271,7 @@
         part_copy(x).start()
         return carry
 
-    lax.fori_loop(0, XS, body, 0)
+    lax.fori_loop(0, XS, body, 0, unroll=True)
     for x in range(XS):
         part_copy(x).wait()
 

time: 62.9 us -> 75.6 us (1.20)
  Pallas kernels: 12.5 us -> 25.2 us
    pallas_call x1, Pallas kernels: 3.02 us -> 15.7 us  [local(): pl.pallas_call(interp_kernel, out_shape=jax.ShapeDtypeStruct((total_field...]
  transfers between devices with their start and end apart: 1 -> 1, of which waited for: 1 -> 1; matrix products, arithmetic and copies ran while one was open for 0% -> 0% of each run, Pallas kernels for 7% -> 5%
where the time goes in v6:
time: 75.6 us; the launch traced here: 74.8 us
  Pallas kernels  25.2 us (33%)
  blocking collectives  20.8 us (28%)
  starting transfers between devices  20.4 us (27%)
  waiting for transfers between devices  7.95 us (11%)
    all_to_all x1, blocking collectives, local(): lax.all_to_all(grid, ('band', 'field'), split_axis=0, concat_axis=0, tile...  20.8 us
    all_to_all x1, starting transfers between devices, local(): lax.all_to_all(four, ('band', 'field'), split_axis=0, concat_axis=0, tile...  20.4 us
    pallas_call x1, Pallas kernels, local(): pl.pallas_call(interp_kernel, out_shape=jax.ShapeDtypeStruct((total_field...  15.7 us
    all_to_all x1, waiting for transfers between devices, local(): lax.all_to_all(four, ('band', 'field'), split_axis=0, concat_axis=0, tile...  7.95 us
    pallas_call x1, Pallas kernels, local(): pl.pallas_call(legendre_kernel, out_shape=jax.ShapeDtypeStruct((bands * J...  4.58 us
    pallas_call x1, Pallas kernels, local(): pl.pallas_call(tables_kernel, out_shape=[jax.ShapeDtypeStruct((waves * pa...  4.07 us
  transfers between devices with their start and end apart: 1, of which 1 were waited for; matrix products, arithmetic and copies ran while one was open for 0% of the time, Pallas kernels for 5%

profile of v6, /device:TPU:1, one launch (start us, length us, event | category | flops | bytes accessed | tf_op | source)
XLA Modules:
  0.0 74.8 jit_solution(49546905247077470)
XLA Ops:
  0.0 0.0 copy-start.4
  0.0 0.0 copy-start.3
  0.0 0.0 copy-start.2
  0.0 0.0 copy-start.1
  0.0 0.0 copy-start
  0.0 4.6 %legendre.1 = bf16[48,4,384]{2,1,0:T(4,128)(2,1)} custom-call(s32[256]{0:T(256)} %wave_hbm.1, bf16[16,2,4,1280]{3,2,1,0:T(4,128)(2,1)} %spec_hbm.1, bf16[16,128,1280]{2,1,0:T(8,128)(2,1)} %leg_hbm.1), custom_call_target="tpu_custom_call" | custom-call | flops 671088640 | bytes 6291456 | tf_op jit(solution)/shard_map/legendre/pallas_call | solution.py:306
  4.6 20.4 %all-to-all-start = ((bf16[48,4,384]{2,1,0:T(4,128)(2,1)}), bf16[48,4,384]{2,1,0:T(4,128)(2,1)S(1)}, u32[]{:S(2)}, u32[]{:S(2)}) async-start(bf16[48,4,384]{2,1,0:T(4,128)(2,1)} %legendre.1), calls=%async_computation | async-start | bytes 294912 | tf_op jit(solution)/shard_map/all_to_all | solution.py:327
  25.1 0.0 copy-done.4
  25.1 0.1 broadcast_in_dim.6
  25.2 0.1 convert_element_type.18.wave_ref
  25.3 0.0 copy-done.3
  25.3 0.0 copy-done.2
  25.4 0.0 copy-done.1
  25.4 0.0 copy-done
  25.4 4.1 %tables.1 = (bf16[512,2048]{1,0:T(8,128)(2,1)S(1)}, f32[50,8,128]{2,1,0:T(8,128)S(1)}) custom-call(f32[512,1]{1,0:T(8,128)S(1)} %convert_element_type.18.wave_ref, f32[1,128]{1,0:T(1,128)S(1)} %fusion.3.start_ref, s32[8,96]{1,0:T(8,128)S(1)} %copy-done, s32[8,96]{1,0:T(8,128)S(1)} %copy-done.1, f32[8,96]{1,0:T(8,128)S(1)} %copy-done.2, f32[8,96]{1,0:T(8,128)S(1)} %copy-done.3), custom_call_target="tpu_custom_call" | custom-call | flops 20971520 | bytes 4194304 | tf_op jit(solution)/shard_map/tables/pallas_call | solution.py:341
  29.5 7.9 %all-to-all-done.four_ref = bf16[48,4,384]{2,1,0:T(4,128)(2,1)S(1)} async-done(((bf16[48,4,384]{2,1,0:T(4,128)(2,1)}), bf16[48,4,384]{2,1,0:T(4,128)(2,1)S(1)}, u32[]{:S(2)}, u32[]{:S(2)}) %all-to-all-start) | async-done | bytes 147488 | tf_op jit(solution)/shard_map/all_to_all | solution.py:327
  37.4 0.8 %fourier.1 = bf16[16,120,128]{2,1,0:T(8,128)(2,1)S(1)} custom-call(bf16[48,4,384]{2,1,0:T(4,128)(2,1)S(1)} %all-to-all-done.four_ref, bf16[512,2048]{1,0:T(8,128)(2,1)S(1)} %get-tuple-element.7.table_ref), custom_call_target="tpu_custom_call" | custom-call | flops 301989888 | bytes 3145728 | tf_op jit(solution)/shard_map/fourier/pallas_call | solution.py:366
  38.2 20.8 %all_to_all.10.grid_ref = bf16[16,120,128]{2,1,0:T(8,128)(2,1)S(1)} all-to-all(bf16[16,120,128]{2,1,0:T(8,128)(2,1)S(1)} %fourier.1), channel_id=1, replica_groups={{0,12,24,36,1,13,25,37,2,14,26,38,3,15,27,39},{4,16,28,40,5,17,29,41,6,..., dimensions={0} | all-to-all | bytes 983040 | tf_op jit(solution)/shard_map/all_to_all | solution.py:380
  59.1 15.7 %interp.1 = f32[192,8,96]{2,1,0:T(8,128)} custom-call(bf16[16,120,128]{2,1,0:T(8,128)(2,1)S(1)} %all_to_all.10.grid_ref, f32[50,8,128]{2,1,0:T(8,128)S(1)} %get-tuple-element.8.taps_ref), custom_call_target="tpu_custom_call" | custom-call | flops 9830400 | bytes 2097152 | tf_op jit(solution)/shard_map/interp/pallas_call | solution.py:384
  (2 shorter events, 0.0 us)
Async XLA Ops:
  0.0 25.1 %copy-start.4 = (s32[256]{0:T(256)S(1)}, s32[256]{0:T(256)}, u32[]{:S(2)}) copy-start(s32[256]{0:T(256)} %wave_hbm.1) | copy-start | bytes 3076
  0.0 25.3 %copy-start.3 = (f32[8,96]{1,0:T(8,128)S(1)}, f32[8,96]{1,0:T(8,128)}, u32[]{:S(2)}) copy-start(f32[8,96]{1,0:T(8,128)} %frac_col.1) | copy-start | bytes 9220
  0.0 25.3 %copy-start.2 = (f32[8,96]{1,0:T(8,128)S(1)}, f32[8,96]{1,0:T(8,128)}, u32[]{:S(2)}) copy-start(f32[8,96]{1,0:T(8,128)} %frac_row.1) | copy-start | bytes 9220
  0.0 25.3 %copy-start.1 = (s32[8,96]{1,0:T(8,128)S(1)}, s32[8,96]{1,0:T(8,128)}, u32[]{:S(2)}) copy-start(s32[8,96]{1,0:T(8,128)} %dep_col.1) | copy-start | bytes 9220
  0.0 25.3 %copy-start = (s32[8,96]{1,0:T(8,128)S(1)}, s32[8,96]{1,0:T(8,128)}, u32[]{:S(2)}) copy-start(s32[8,96]{1,0:T(8,128)} %dep_row.1) | copy-start | bytes 9220
  4.6 32.8 %all-to-all-start = ((bf16[48,4,384]{2,1,0:T(4,128)(2,1)}), bf16[48,4,384]{2,1,0:T(4,128)(2,1)S(1)}, u32[]{:S(2)}, u32[]{:S(2)}) async-start(bf16[48,4,384]{2,1,0:T(4,128)(2,1)} %legendre.1), calls=%async_computation | async-start | bytes 294912 | tf_op jit(solution)/shard_map/all_to_all | solution.py:327

commit v7 on v6

--- a/solution.py
+++ b/solution.py
@@ -271,7 +271,7 @@
         part_copy(x).start()
         return carry
 
-    lax.fori_loop(0, XS, body, 0, unroll=True)
+    lax.fori_loop(0, XS, body, 0)
     for x in range(XS):
         part_copy(x).wait()
 

time: 75.6 us -> 62.4 us (0.83)
  Pallas kernels: 25.2 us -> 12 us
    pallas_call x1, Pallas kernels: 15.7 us -> 2.55 us  [local(): pl.pallas_call(interp_kernel, out_shape=jax.ShapeDtypeStruct((total_field...]
  transfers between devices with their start and end apart: 1 -> 1, of which waited for: 1 -> 1; matrix products, arithmetic and copies ran while one was open for 0% -> 0% of each run, Pallas kernels for 5% -> 7%
where the time goes in v7:
time: 62.4 us; the launch traced here: 61.6 us
  blocking collectives  20.8 us (33%)
  starting transfers between devices  20.4 us (33%)
  Pallas kernels  12 us (19%)
  waiting for transfers between devices  7.95 us (13%)
    all_to_all x1, blocking collectives, local(): lax.all_to_all(grid, ('band', 'field'), split_axis=0, concat_axis=0, tile...  20.8 us
    all_to_all x1, starting transfers between devices, local(): lax.all_to_all(four, ('band', 'field'), split_axis=0, concat_axis=0, tile...  20.4 us
    all_to_all x1, waiting for transfers between devices, local(): lax.all_to_all(four, ('band', 'field'), split_axis=0, concat_axis=0, tile...  7.95 us
    pallas_call x1, Pallas kernels, local(): pl.pallas_call(legendre_kernel, out_shape=jax.ShapeDtypeStruct((bands * J...  4.58 us
    pallas_call x1, Pallas kernels, local(): pl.pallas_call(tables_kernel, out_shape=[jax.ShapeDtypeStruct((waves * pa...  4.07 us
    pallas_call x1, Pallas kernels, local(): pl.pallas_call(interp_kernel, out_shape=jax.ShapeDtypeStruct((total_field...  2.55 us
  transfers between devices with their start and end apart: 1, of which 1 were waited for; matrix products, arithmetic and copies ran while one was open for 0% of the time, Pallas kernels for 7%

profile of v7, /device:TPU:1, one launch (start us, length us, event | category | flops | bytes accessed | tf_op | source)
XLA Modules:
  0.0 61.6 jit_solution(6540665494379323767)
XLA Ops:
  0.0 0.0 copy-start.4
  0.0 0.0 copy-start.3
  0.0 0.0 copy-start.2
  0.0 0.0 copy-start.1
  0.0 0.0 copy-start
  0.0 4.6 %legendre.1 = bf16[48,4,384]{2,1,0:T(4,128)(2,1)} custom-call(s32[256]{0:T(256)} %wave_hbm.1, bf16[16,2,4,1280]{3,2,1,0:T(4,128)(2,1)} %spec_hbm.1, bf16[16,128,1280]{2,1,0:T(8,128)(2,1)} %leg_hbm.1), custom_call_target="tpu_custom_call" | custom-call | flops 671088640 | bytes 6291456 | tf_op jit(solution)/shard_map/legendre/pallas_call | solution.py:306
  4.6 20.4 %all-to-all-start = ((bf16[48,4,384]{2,1,0:T(4,128)(2,1)}), bf16[48,4,384]{2,1,0:T(4,128)(2,1)S(1)}, u32[]{:S(2)}, u32[]{:S(2)}) async-start(bf16[48,4,384]{2,1,0:T(4,128)(2,1)} %legendre.1), calls=%async_computation | async-start | bytes 294912 | tf_op jit(solution)/shard_map/all_to_all | solution.py:327
  25.1 0.0 copy-done.4
  25.1 0.1 broadcast_in_dim.6
  25.2 0.1 convert_element_type.18.wave_ref
  25.3 0.0 copy-done.3
  25.3 0.0 copy-done.2
  25.4 0.0 copy-done.1
  25.4 0.0 copy-done
  25.4 4.1 %tables.1 = (bf16[512,2048]{1,0:T(8,128)(2,1)S(1)}, f32[50,8,128]{2,1,0:T(8,128)S(1)}) custom-call(f32[512,1]{1,0:T(8,128)S(1)} %convert_element_type.18.wave_ref, f32[1,128]{1,0:T(1,128)S(1)} %fusion.3.start_ref, s32[8,96]{1,0:T(8,128)S(1)} %copy-done, s32[8,96]{1,0:T(8,128)S(1)} %copy-done.1, f32[8,96]{1,0:T(8,128)S(1)} %copy-done.2, f32[8,96]{1,0:T(8,128)S(1)} %copy-done.3), custom_call_target="tpu_custom_call" | custom-call | flops 20971520 | bytes 4194304 | tf_op jit(solution)/shard_map/tables/pallas_call | solution.py:341
  29.5 7.9 %all-to-all-done.four_ref = bf16[48,4,384]{2,1,0:T(4,128)(2,1)S(1)} async-done(((bf16[48,4,384]{2,1,0:T(4,128)(2,1)}), bf16[48,4,384]{2,1,0:T(4,128)(2,1)S(1)}, u32[]{:S(2)}, u32[]{:S(2)}) %all-to-all-start) | async-done | bytes 147488 | tf_op jit(solution)/shard_map/all_to_all | solution.py:327
  37.4 0.8 %fourier.1 = bf16[16,120,128]{2,1,0:T(8,128)(2,1)S(1)} custom-call(bf16[48,4,384]{2,1,0:T(4,128)(2,1)S(1)} %all-to-all-done.four_ref, bf16[512,2048]{1,0:T(8,128)(2,1)S(1)} %get-tuple-element.7.table_ref), custom_call_target="tpu_custom_call" | custom-call | flops 301989888 | bytes 3145728 | tf_op jit(solution)/shard_map/fourier/pallas_call | solution.py:366
  38.2 20.8 %all_to_all.10.grid_ref = bf16[16,120,128]{2,1,0:T(8,128)(2,1)S(1)} all-to-all(bf16[16,120,128]{2,1,0:T(8,128)(2,1)S(1)} %fourier.1), channel_id=1, replica_groups={{0,12,24,36,1,13,25,37,2,14,26,38,3,15,27,39},{4,16,28,40,5,17,29,41,6,..., dimensions={0} | all-to-all | bytes 983040 | tf_op jit(solution)/shard_map/all_to_all | solution.py:380
  59.1 2.6 %interp.1 = f32[192,8,96]{2,1,0:T(8,128)} custom-call(bf16[16,120,128]{2,1,0:T(8,128)(2,1)S(1)} %all_to_all.10.grid_ref, f32[50,8,128]{2,1,0:T(8,128)S(1)} %get-tuple-element.8.taps_ref), custom_call_target="tpu_custom_call" | custom-call | flops 9830400 | bytes 2097152 | tf_op jit(solution)/shard_map/interp/pallas_call | solution.py:384
  (2 shorter events, 0.0 us)
Async XLA Ops:
  0.0 25.1 %copy-start.4 = (s32[256]{0:T(256)S(1)}, s32[256]{0:T(256)}, u32[]{:S(2)}) copy-start(s32[256]{0:T(256)} %wave_hbm.1) | copy-start | bytes 3076
  0.0 25.3 %copy-start.3 = (f32[8,96]{1,0:T(8,128)S(1)}, f32[8,96]{1,0:T(8,128)}, u32[]{:S(2)}) copy-start(f32[8,96]{1,0:T(8,128)} %frac_col.1) | copy-start | bytes 9220
  0.0 25.3 %copy-start.2 = (f32[8,96]{1,0:T(8,128)S(1)}, f32[8,96]{1,0:T(8,128)}, u32[]{:S(2)}) copy-start(f32[8,96]{1,0:T(8,128)} %frac_row.1) | copy-start | bytes 9220
  0.0 25.3 %copy-start.1 = (s32[8,96]{1,0:T(8,128)S(1)}, s32[8,96]{1,0:T(8,128)}, u32[]{:S(2)}) copy-start(s32[8,96]{1,0:T(8,128)} %dep_col.1) | copy-start | bytes 9220
  0.0 25.3 %copy-start = (s32[8,96]{1,0:T(8,128)S(1)}, s32[8,96]{1,0:T(8,128)}, u32[]{:S(2)}) copy-start(s32[8,96]{1,0:T(8,128)} %dep_row.1) | copy-start | bytes 9220
  4.6 32.8 %all-to-all-start = ((bf16[48,4,384]{2,1,0:T(4,128)(2,1)}), bf16[48,4,384]{2,1,0:T(4,128)(2,1)S(1)}, u32[]{:S(2)}, u32[]{:S(2)}) async-start(bf16[48,4,384]{2,1,0:T(4,128)(2,1)} %legendre.1), calls=%async_computation | async-start | bytes 294912 | tf_op jit(solution)/shard_map/all_to_all | solution.py:327
